TPU v7x, 128 devices: a whole 4x4x4 slice. The times are simulated.
128 devices in a mesh: patch: 16 (over z, x), exp: 8 (over y, core).
Axes of the slice: x: 4, y: 4, z: 4, core: 2. Of those that a mesh axis runs over, the one named last changes fastest.
Arguments:
- sky_model: float32 [16, 8, 6, 256, 256], P('patch', 'exp'), may hold values from -6 to 6
- stamp_pixels: bfloat16 [16384, 256, 256], P(('patch', 'exp')), may hold values from -6 to 6
- stamp_patch: int32 [16384, 1], P(('patch', 'exp')), may hold values from 0 to 15; in each aligned block of 128 rows (0 to 127, 128 to 255, ...) at most 12 rows name the same one
- stamp_band: int32 [16384], P(('patch', 'exp')), may hold values from 0 to 5
- psf_taps: bfloat16 [16384, 2, 21], P(('patch', 'exp')), may hold values from 0.019897461 to 0.19921875
- stamp_gain: bfloat16 [16384], P(('patch', 'exp')), may hold values from 0.5 to 2
- stamp_weight: bfloat16 [16384], P(('patch', 'exp')), may hold values from 0.25 to 4
Outputs:
- new_model: float32 [16, 8, 6, 256, 256], P('patch', 'exp')
- step_rms: float32 [], replicated
Inputs may be any that keep to these rules, and one draw needn't show every extreme that they name: `stamp_patch`: among the stamps of one device no patch is named by more than 12 stamps, a bound that some block reaches.
All inputs are finite; a program needn't handle non-finite values.
Results may differ from a plain program's by a relative error of at most 0.013.
Values may be sent and summed in bfloat16 or wider, within the bound.
A program may use at most 192 MiB of HBM per device.

v0:
```python
import jax
import jax.numpy as jnp
from jax import lax
from jax.sharding import PartitionSpec as P

step_rate = 0.2


def banded_matrices(tap_values, tile_size):
    tap_length = tap_values.shape[-1]
    half_width = (tap_length - 1) // 2
    pixel_index = jnp.arange(tile_size, dtype=jnp.int32)
    offset = pixel_index[None, :] - pixel_index[:, None] + half_width
    tap_table = (
        offset[None, :, :] == jnp.arange(tap_length, dtype=jnp.int32)[:, None, None]
    ).astype(jnp.bfloat16)
    return jnp.einsum(
        "sk,kij->sij", tap_values, tap_table, preferred_element_type=jnp.float32
    ).astype(jnp.bfloat16)


def stamp_adjoint(tile_sel, pixels, tap_values, gain_rows, weight_rows):
    tile_size = pixels.shape[-1]
    row_kernel = banded_matrices(tap_values[:, 0], tile_size)
    col_kernel = banded_matrices(tap_values[:, 1], tile_size)
    blurred = jnp.einsum(
        "sab,scb->sac", tile_sel, col_kernel, preferred_element_type=jnp.float32
    ).astype(jnp.bfloat16)
    gain_wide = gain_rows.astype(jnp.float32)[:, None, None]
    predicted = gain_wide * jnp.einsum(
        "sab,sbc->sac", row_kernel, blurred, preferred_element_type=jnp.float32
    )
    residual = (
        weight_rows.astype(jnp.float32)[:, None, None] * (predicted - pixels.astype(jnp.float32))
    ).astype(jnp.bfloat16)
    backward = jnp.einsum(
        "sba,sbc->sac", row_kernel, residual, preferred_element_type=jnp.float32
    ).astype(jnp.bfloat16)
    return gain_wide * jnp.einsum(
        "sab,sbc->sac", backward, col_kernel, preferred_element_type=jnp.float32
    )


def per_device(
    sky_model, stamp_pixels, stamp_patch, stamp_band, psf_taps, stamp_gain, stamp_weight
):
    band_count = sky_model.shape[2]
    tile_size = sky_model.shape[-1]
    stamp_count = stamp_pixels.shape[0]
    tap_length = psf_taps.shape[-1]
    block_rows = 32
    model_half = sky_model.astype(jnp.bfloat16)
    patches = lax.axis_size("patch")
    gathered = lax.all_gather(model_half, "patch", axis=0, tiled=True)
    key_count = gathered.shape[0] * band_count
    flat_tiles = gathered.reshape(key_count, tile_size, tile_size)
    tile_keys = stamp_patch[:, 0] * band_count + stamp_band
    block_count = stamp_count // block_rows
    block_inputs = (
        stamp_pixels.reshape(block_count, block_rows, tile_size, tile_size),
        tile_keys.reshape(block_count, block_rows),
        psf_taps.reshape(block_count, block_rows, 2, tap_length),
        stamp_gain.reshape(block_count, block_rows),
        stamp_weight.reshape(block_count, block_rows),
    )

    def source_block(running, block_parts):
        pixels, keys_block, tap_values, gain_rows, weight_rows = block_parts
        tile_sel = jnp.take(flat_tiles, keys_block, axis=0)
        adjoint = stamp_adjoint(tile_sel, pixels, tap_values, gain_rows, weight_rows)
        return (running.at[keys_block].add(adjoint), None)

    result = lax.scan(
        source_block, jnp.zeros((key_count, tile_size, tile_size), jnp.float32), block_inputs
    )
    gradient = lax.psum_scatter(
        result[0].reshape(gathered.shape).astype(jnp.bfloat16),
        "patch",
        scatter_dimension=0,
        tiled=True,
    ).astype(jnp.float32)
    step_field = step_rate * gradient
    new_model = sky_model - step_field
    square_sum = lax.psum(jnp.sum(step_field * step_field), ("patch", "exp"))
    entry_count = patches * lax.axis_size("exp") * band_count * tile_size * tile_size
    step_rms = jnp.sqrt(square_sum / entry_count + 1e-06)
    return (new_model, step_rms)


def solution(mesh):
    return jax.shard_map(
        per_device,
        mesh=mesh,
        in_specs=(
            P("patch", "exp", None, None, None),
            P(("patch", "exp"), None, None),
            P(("patch", "exp"), None),
            P(("patch", "exp")),
            P(("patch", "exp"), None, None),
            P(("patch", "exp")),
            P(("patch", "exp")),
        ),
        out_specs=(P("patch", "exp", None, None, None), P()),
        check_vma=False,
    )
```

profile of v0, /device:TPU:1, one launch (start us, length us, event | category | flops | bytes accessed | tf_op | source)
XLA Modules:
  0.0 557.4 jit_solution(9071368639380420495)
XLA Ops:
  12.7 91.4 %all-gather.2.cloned.1.call-done = bf16[16,1,6,256,256]{4,3,2,1,0:T(8,128)(2,1)} async-done(((bf16[1,1,6,256,256]{4,3,2,1,0:T(8,128)(2,1)}), bf16[16,1,6,256,256]{4,3,2,1,0:T(8,128)(2,1)}) %all-gather.2.cloned.1.call-update) | async-done | bytes 12582928 | tf_op jit(solution)/shard_map/all_gather | solution.py:54
  104.1 11.4 %broadcast_in_dim.12 = f32[96,256,256]{2,1,0:T(8,128)} broadcast(f32[]{:T(128)} %constant.24.clone.1), dimensions={} | broadcast | bytes 25165828 | tf_op jit(solution)/shard_map/broadcast_in_dim | solution.py:74
  115.5 258.4 %while.10 = (s32[]{:T(128)}, f32[96,256,256]{2,1,0:T(8,128)}, s32[4,32]{1,0:T(4,128)S(1)}, bf16[4,32]{1,0:T(4,128)(2,1)S(1)}, bf16[4,32,2,21]{1,3,2,0:T(8,128)(2...) while((s32[]{:T(128)}, f32[96,256,256]{2,1,0:T(8,128)}, ...), condition=%wide.region_2.3_spmd, body=%wide.region_0.2_spmd.sunk | while | flops 4494984704 | bytes 135027696 | solution.py:73
  115.6 7.3 %gather_fusion = bf16[32,256,256]{2,1,0:T(8,128)(2,1)} fusion(bf16[96,256,256]{2,1,0:T(8,128)(2,1)} %get-tuple-element.158, s32[1024]{0:T(1024)S(1)} %pad_clamp_fusion.2), kind=kCustom, calls=%fused_computation.clone.1 | custom fusion | bytes 8388736 | tf_op jit(solution)/shard_map/while/body/eval_jaxpr/jit(_take)/gather | solution.py:69
  125.2 5.0 fusion.70
  130.2 3.3 fusion.69
  133.5 7.5 %copy.28 = bf16[32,256,256]{1,2,0:T(8,128)(2,1)} copy(bf16[32,256,256]{2,0,1:T(8,128)(2,1)} %fusion.69) | data formatting | bytes 8388608 | tf_op jit(solution)/shard_map/while/body/eval_jaxpr/convert_element_type | solution.py:19
  141.0 10.6 %fusion.71 = bf16[32,256,256]{2,1,0:T(8,128)(2,1)} fusion(bf16[32,256,256]{1,2,0:T(8,128)(2,1)} %copy.28, bf16[4,32,256,256]{3,2,1,0:T(8,128)(2,1)} %get-tuple-element.159, s32[]{:T(128)S(6)} %copy.32, f32[32]{0:T(128)S(1)} %get-tuple-element.133, f32[32]{0:T(128)S(1)} %get-tuple-element.132, bf16[32,256,256]{2,1,0:T(8,128)(2,1)} %fusion.70), kind=kOutput, calls=%fused_computation.8.clone.1 | convolution fusion | flops 2157969408 | bytes 20971780 | tf_op jit(solution)/shard_map/while/body/eval_jaxpr/sba,sbc->sac/dot_general | solution.py:36
  151.7 9.6 %broadcast_multiply_fusion.2 = f32[32,256,256]{2,1,0:T(8,128)} fusion(f32[32]{0:T(128)S(1)} %get-tuple-element.132, bf16[32,256,256]{2,0,1:T(8,128)(2,1)} %copy-done, bf16[32,256,256]{2,1,0:T(8,128)(2,1)} %fusion.71), kind=kOutput, calls=%fused_computation.18.clone.1 | convolution fusion | flops 1075838976 | bytes 16777344 | tf_op jit(solution)/shard_map/while/body/eval_jaxpr/sab,sbc->sac/dot_general | solution.py:39
  161.2 18.9 %scatter_fusion = f32[96,256,256]{2,1,0:T(8,128)} fusion(f32[96,256,256]{2,1,0:T(8,128)} %get-tuple-element.144, s32[32]{0:T(128)S(1)} %fusion.66, f32[32,256,256]{2,1,0:T(8,128)} %broadcast_multiply_fusion.2), kind=kCustom, calls=%fused_computation.1.clone.1 | custom fusion | flops 2097152 | bytes 25165952 | tf_op jit(solution)/shard_map/while/body/eval_jaxpr/scatter-add | solution.py:71
  180.2 7.3 %gather_fusion = bf16[32,256,256]{2,1,0:T(8,128)(2,1)} fusion(bf16[96,256,256]{2,1,0:T(8,128)(2,1)} %get-tuple-element.158, s32[1024]{0:T(1024)S(1)} %pad_clamp_fusion.2), kind=kCustom, calls=%fused_computation.clone.1 | custom fusion | bytes 8388736 | tf_op jit(solution)/shard_map/while/body/eval_jaxpr/jit(_take)/gather | solution.py:69
  189.7 5.0 fusion.70
  194.7 3.3 fusion.69
  198.0 7.5 %copy.28 = bf16[32,256,256]{1,2,0:T(8,128)(2,1)} copy(bf16[32,256,256]{2,0,1:T(8,128)(2,1)} %fusion.69) | data formatting | bytes 8388608 | tf_op jit(solution)/shard_map/while/body/eval_jaxpr/convert_element_type | solution.py:19
  205.6 10.6 %fusion.71 = bf16[32,256,256]{2,1,0:T(8,128)(2,1)} fusion(bf16[32,256,256]{1,2,0:T(8,128)(2,1)} %copy.28, bf16[4,32,256,256]{3,2,1,0:T(8,128)(2,1)} %get-tuple-element.159, s32[]{:T(128)S(6)} %copy.32, f32[32]{0:T(128)S(1)} %get-tuple-element.133, f32[32]{0:T(128)S(1)} %get-tuple-element.132, bf16[32,256,256]{2,1,0:T(8,128)(2,1)} %fusion.70), kind=kOutput, calls=%fused_computation.8.clone.1 | convolution fusion | flops 2157969408 | bytes 20971780 | tf_op jit(solution)/shard_map/while/body/eval_jaxpr/sba,sbc->sac/dot_general | solution.py:36
  216.2 9.6 %broadcast_multiply_fusion.2 = f32[32,256,256]{2,1,0:T(8,128)} fusion(f32[32]{0:T(128)S(1)} %get-tuple-element.132, bf16[32,256,256]{2,0,1:T(8,128)(2,1)} %copy-done, bf16[32,256,256]{2,1,0:T(8,128)(2,1)} %fusion.71), kind=kOutput, calls=%fused_computation.18.clone.1 | convolution fusion | flops 1075838976 | bytes 16777344 | tf_op jit(solution)/shard_map/while/body/eval_jaxpr/sab,sbc->sac/dot_general | solution.py:39
  225.8 19.1 %scatter_fusion = f32[96,256,256]{2,1,0:T(8,128)} fusion(f32[96,256,256]{2,1,0:T(8,128)} %get-tuple-element.144, s32[32]{0:T(128)S(1)} %fusion.66, f32[32,256,256]{2,1,0:T(8,128)} %broadcast_multiply_fusion.2), kind=kCustom, calls=%fused_computation.1.clone.1 | custom fusion | flops 2097152 | bytes 25165952 | tf_op jit(solution)/shard_map/while/body/eval_jaxpr/scatter-add | solution.py:71
  244.9 7.3 %gather_fusion = bf16[32,256,256]{2,1,0:T(8,128)(2,1)} fusion(bf16[96,256,256]{2,1,0:T(8,128)(2,1)} %get-tuple-element.158, s32[1024]{0:T(1024)S(1)} %pad_clamp_fusion.2), kind=kCustom, calls=%fused_computation.clone.1 | custom fusion | bytes 8388736 | tf_op jit(solution)/shard_map/while/body/eval_jaxpr/jit(_take)/gather | solution.py:69
  254.5 5.0 fusion.70
  262.8 7.5 %copy.28 = bf16[32,256,256]{1,2,0:T(8,128)(2,1)} copy(bf16[32,256,256]{2,0,1:T(8,128)(2,1)} %fusion.69) | data formatting | bytes 8388608 | tf_op jit(solution)/shard_map/while/body/eval_jaxpr/convert_element_type | solution.py:19
  270.3 10.6 %fusion.71 = bf16[32,256,256]{2,1,0:T(8,128)(2,1)} fusion(bf16[32,256,256]{1,2,0:T(8,128)(2,1)} %copy.28, bf16[4,32,256,256]{3,2,1,0:T(8,128)(2,1)} %get-tuple-element.159, s32[]{:T(128)S(6)} %copy.32, f32[32]{0:T(128)S(1)} %get-tuple-element.133, f32[32]{0:T(128)S(1)} %get-tuple-element.132, bf16[32,256,256]{2,1,0:T(8,128)(2,1)} %fusion.70), kind=kOutput, calls=%fused_computation.8.clone.1 | convolution fusion | flops 2157969408 | bytes 20971780 | tf_op jit(solution)/shard_map/while/body/eval_jaxpr/sba,sbc->sac/dot_general | solution.py:36
  280.9 9.6 %broadcast_multiply_fusion.2 = f32[32,256,256]{2,1,0:T(8,128)} fusion(f32[32]{0:T(128)S(1)} %get-tuple-element.132, bf16[32,256,256]{2,0,1:T(8,128)(2,1)} %copy-done, bf16[32,256,256]{2,1,0:T(8,128)(2,1)} %fusion.71), kind=kOutput, calls=%fused_computation.18.clone.1 | convolution fusion | flops 1075838976 | bytes 16777344 | tf_op jit(solution)/shard_map/while/body/eval_jaxpr/sab,sbc->sac/dot_general | solution.py:39
  290.5 19.0 %scatter_fusion = f32[96,256,256]{2,1,0:T(8,128)} fusion(f32[96,256,256]{2,1,0:T(8,128)} %get-tuple-element.144, s32[32]{0:T(128)S(1)} %fusion.66, f32[32,256,256]{2,1,0:T(8,128)} %broadcast_multiply_fusion.2), kind=kCustom, calls=%fused_computation.1.clone.1 | custom fusion | flops 2097152 | bytes 25165952 | tf_op jit(solution)/shard_map/while/body/eval_jaxpr/scatter-add | solution.py:71
  309.6 7.3 %gather_fusion = bf16[32,256,256]{2,1,0:T(8,128)(2,1)} fusion(bf16[96,256,256]{2,1,0:T(8,128)(2,1)} %get-tuple-element.158, s32[1024]{0:T(1024)S(1)} %pad_clamp_fusion.2), kind=kCustom, calls=%fused_computation.clone.1 | custom fusion | bytes 8388736 | tf_op jit(solution)/shard_map/while/body/eval_jaxpr/jit(_take)/gather | solution.py:69
  319.1 5.0 fusion.70
  327.4 7.5 %copy.28 = bf16[32,256,256]{1,2,0:T(8,128)(2,1)} copy(bf16[32,256,256]{2,0,1:T(8,128)(2,1)} %fusion.69) | data formatting | bytes 8388608 | tf_op jit(solution)/shard_map/while/body/eval_jaxpr/convert_element_type | solution.py:19
  334.9 10.6 %fusion.71 = bf16[32,256,256]{2,1,0:T(8,128)(2,1)} fusion(bf16[32,256,256]{1,2,0:T(8,128)(2,1)} %copy.28, bf16[4,32,256,256]{3,2,1,0:T(8,128)(2,1)} %get-tuple-element.159, s32[]{:T(128)S(6)} %copy.32, f32[32]{0:T(128)S(1)} %get-tuple-element.133, f32[32]{0:T(128)S(1)} %get-tuple-element.132, bf16[32,256,256]{2,1,0:T(8,128)(2,1)} %fusion.70), kind=kOutput, calls=%fused_computation.8.clone.1 | convolution fusion | flops 2157969408 | bytes 20971780 | tf_op jit(solution)/shard_map/while/body/eval_jaxpr/sba,sbc->sac/dot_general | solution.py:36
  345.6 9.6 %broadcast_multiply_fusion.2 = f32[32,256,256]{2,1,0:T(8,128)} fusion(f32[32]{0:T(128)S(1)} %get-tuple-element.132, bf16[32,256,256]{2,0,1:T(8,128)(2,1)} %copy-done, bf16[32,256,256]{2,1,0:T(8,128)(2,1)} %fusion.71), kind=kOutput, calls=%fused_computation.18.clone.1 | convolution fusion | flops 1075838976 | bytes 16777344 | tf_op jit(solution)/shard_map/while/body/eval_jaxpr/sab,sbc->sac/dot_general | solution.py:39
  355.2 18.7 %scatter_fusion = f32[96,256,256]{2,1,0:T(8,128)} fusion(f32[96,256,256]{2,1,0:T(8,128)} %get-tuple-element.144, s32[32]{0:T(128)S(1)} %fusion.66, f32[32,256,256]{2,1,0:T(8,128)} %broadcast_multiply_fusion.2), kind=kCustom, calls=%fused_computation.1.clone.1 | custom fusion | flops 2097152 | bytes 25165952 | tf_op jit(solution)/shard_map/while/body/eval_jaxpr/scatter-add | solution.py:71
  373.9 13.2 %convert_element_type.64 = bf16[96,256,256]{2,1,0:T(8,128)(2,1)} convert(f32[96,256,256]{2,1,0:T(8,128)} %get-tuple-element.44) | non-fusion elementwise | flops 6291456 | bytes 37748736 | tf_op jit(solution)/shard_map/convert_element_type | solution.py:77
  387.1 93.9 %reduce-scatter.4.cloned.1.call-done = bf16[1,1,6,256,256]{4,3,2,1,0:T(8,128)(2,1)} async-done(((bf16[16,1,6,256,256]{4,3,2,1,0:T(8,128)(2,1)}), bf16[1,1,6,256,256]{4,3,2,1,0:T(8,128)(2,1)}) %reduce-scatter.4.cloned.1.call-update) | async-done | bytes 786448
  484.3 64.5 %psum.7 = f32[]{:T(128)} all-reduce(f32[]{:T(128)} %get-tuple-element.79), channel_id=1, replica_groups=mesh['patch'=16,'exp'=8] {'patch','exp'}, use_global_device_ids=true, to_apply=%region_5.6 | all-reduce | flops 1 | bytes 8 | tf_op jit(solution)/shard_map/psum | solution.py:84
  (60 shorter events, 24.4 us)
Async XLA Ops:
  7.2 96.9 %all-gather.2.cloned.1.call-start = ((), (), s32[]{:S(2)}) async-start(), calls=%async_computation.1 | async-start | bytes 13369344 | tf_op jit(solution)/shard_map/all_gather | solution.py:54
  9.6 471.4 %reduce-scatter.4.cloned.1.call-start = ((), (), s32[]{:S(2)}) async-start(), calls=%async_computation.2 | async-start | bytes 13369344
  123.0 2.2 copy-start.1
  125.2 5.0 copy-start
  187.5 2.2 copy-start.1
  189.7 5.0 copy-start
  252.3 2.2 copy-start.1
  254.5 5.0 copy-start
  316.9 2.2 copy-start.1
  319.1 5.0 copy-start
  387.1 94.0 %copy-start.2 = (f32[1,1,6,256,256]{4,3,2,1,0:T(8,128)S(1)}, f32[1,1,6,256,256]{4,3,2,1,0:T(8,128)}, u32[]{:S(2)}) copy-start(f32[1,1,6,256,256]{4,3,2,1,0:T(8,128)} %param.9) | copy-start | bytes 4718596
Sparse Core Ops, SparseCore 0:
  10.7 93.3 all-gather.1
  387.2 93.7 reduce-scatter.3
where the time goes:
time: 559 us; the launch traced here: 557 us
  waiting for transfers between devices  185 us (33%)
  matrix products  119 us (21%)
  other arithmetic  95.3 us (17%)
  local copies, waits for them, and re-layouts  77 us (14%)
  blocking collectives  64.5 us (12%)
  between operations  15.9 us (3%)
    unnamed x3, waiting for transfers between devices  94 us
    all_gather x1, waiting for transfers between devices, per_device(): gathered = lax.all_gather(model_half, 'patch', axis=0, tiled=True)  91.4 us
    scatter-add x4, other arithmetic, source_block(): return (running.at[keys_block].add(adjoint), None)  75.6 us
    psum x1, blocking collectives, per_device(): square_sum = lax.psum(jnp.sum(step_field * step_field), ('patch', 'exp'))  64.5 us
    dot_general x4, matrix products, stamp_adjoint(): jnp.einsum('sba,sbc->sac', row_kernel, residual, preferred_element_type=j...  42.6 us
    dot_general x4, matrix products, stamp_adjoint(): jnp.einsum('sab,sbc->sac', backward, col_kernel, preferred_element_type=j...  38.3 us
    convert_element_type x4, local copies, waits for them, and re-layouts, banded_matrices(): return jnp.einsum('sk,kij->sij', tap_values, tap_table, preferred_element...  30.1 us
    gather x4, local copies, waits for them, and re-layouts, source_block(): tile_sel = jnp.take(flat_tiles, keys_block, axis=0)  29.4 us
  transfers between devices with their start and end apart: 2, of which 2 were waited for; matrix products, arithmetic and copies ran while one was open for 1% of the time, Pallas kernels for 0%

commit v1 on v0

v1 whole, which is shorter than its diff:
```python
import functools

import jax
import jax.numpy as jnp
from jax import lax
from jax.experimental import pallas as pl
from jax.experimental.pallas import tpu as pltpu
from jax.sharding import PartitionSpec as P

TS = 256
BANDS = 6
HALF = 3
STAMPS = 128
STEP_RATE = 0.2
F32, BF16 = jnp.float32, jnp.bfloat16
MESH = pl.DeviceIdType.MESH

UNITS = [
    (0, 0), (0, 1), (0, -1), (1, 0), (-1, 0),
    (0, 2), (2, 0), (1, 1), (1, -1), (-1, 1), (-1, -1),
    (2, 1), (2, -1), (1, 2), (-1, 2), (2, 2),
]
UNIT = {offset: number for number, offset in enumerate(UNITS)}
GROUPS = [(0, 5), (5, 11), (11, 16)]
LINKS = [(0, 1), (0, -1), (1, 0), (-1, 0)]


def place_on_torus():
    patch = lax.axis_index("patch")
    return patch // 4, lax.rem(patch, 4)


def neighbour(offset):
    z, x = place_on_torus()
    return lax.rem(z + offset[0] + 4, 4) * 4 + lax.rem(x + offset[1] + 4, 4)


def from_offset(value, offset):
    dz, dx = offset
    pairs = [
        (((z + dz) % 4) * 4 + (x + dx) % 4, z * 4 + x) for z in range(4) for x in range(4)
    ]
    return lax.ppermute(value, "patch", pairs)


def gather_units(low, high):
    first = {(0, 0): (low, high)}
    for link in LINKS[:2]:
        first[link] = [from_offset(low, link)]
    for link in LINKS[2:]:
        first[link] = [from_offset(high, link)]
    for link in LINKS[:2]:
        first[link].append(from_offset(high, link))
    for link in LINKS[2:]:
        first[link].insert(0, from_offset(low, link))
    units = dict(first)
    for dz in (1, -1):
        for dx in (1, -1):
            units[dz, dx] = (
                from_offset(first[0, dx][0], (dz, 0)),
                from_offset(first[dz, 0][1], (0, dx)),
            )
    units[0, 2] = (from_offset(first[0, 1][0], (0, 1)), from_offset(first[0, -1][1], (0, -1)))
    units[2, 0] = (from_offset(first[1, 0][0], (1, 0)), from_offset(first[-1, 0][1], (-1, 0)))
    for d in (1, -1):
        units[2, d] = tuple(from_offset(part, (0, d)) for part in units[2, 0])
        units[d, 2] = tuple(from_offset(part, (d, 0)) for part in units[0, 2])
    out = {k: [(v[0], 0, 0), (v[1], HALF, 0)] for k, v in units.items()}
    out[2, 2] = []
    for quarter, link in enumerate(LINKS):
        via = tuple(2 if d == 0 else d for d in link)
        rows = slice(quarter * 64, quarter * 64 + 64)
        part = jnp.concatenate([p[:, rows] for p in units[via]], 0)
        out[2, 2].append((from_offset(part, link), 0, quarter * 64))
    return out


def tap_rows(taps):
    half = taps.shape[-1] // 2

    def ring(v):
        gap = jnp.zeros(v.shape[:-1] + (128 - v.shape[-1],), v.dtype)
        return jnp.concatenate([v[..., half:], gap, v[..., :half]], -1)

    both = jnp.stack([ring(taps), ring(taps[..., ::-1])], 2)
    both = both.reshape(taps.shape[0], 4, 128).astype(F32)
    return jnp.pad(both, ((0, 0), (0, 4), (0, 0)))


def stamp_order(stamp_patch, stamp_band):
    z, x = place_on_torus()
    dz = lax.rem(stamp_patch // 4 - z + 4, 4)
    dx = lax.rem(lax.rem(stamp_patch, 4) - x + 4, 4)
    offset = dz * 4 + dx
    unit = jnp.zeros_like(offset)
    for number, (a, b) in enumerate(UNITS):
        unit = jnp.where(offset == (a % 4) * 4 + b % 4, number, unit)
    group = (unit >= GROUPS[1][0]).astype(jnp.int32) + (unit >= GROUPS[2][0]).astype(jnp.int32)
    base = jnp.where(group == 0, 0, jnp.where(group == 1, GROUPS[1][0], GROUPS[2][0]))
    tile = (unit - base) * BANDS + stamp_band
    number = jnp.arange(STAMPS, dtype=jnp.int32)
    rank = group * STAMPS + number
    spot = jnp.sum((rank[None, :] < rank[:, None]).astype(jnp.int32), 1)
    here = spot[None, :] == jnp.arange(STAMPS + 8, dtype=jnp.int32)[:, None]
    ids = jnp.sum(jnp.where(here, number[None, :], 0), 1)
    tiles = jnp.sum(jnp.where(here, tile[None, :], 0), 1)
    bounds = jnp.sum((group[None, :] < jnp.arange(4, dtype=jnp.int32)[:, None]).astype(jnp.int32), 1)
    return ids, tiles, bounds


def build(row, dst):
    ring = pltpu.roll(jnp.broadcast_to(row, (128, 128)), 0, 1, stride=1, stride_axis=0)
    d = lax.broadcasted_iota(jnp.int32, (128, 128), 1) - lax.broadcasted_iota(
        jnp.int32, (128, 128), 0
    )
    zero = jnp.zeros_like(ring)
    diag = jnp.where(jnp.abs(d) < 64, ring, zero).astype(BF16)
    dst[0:128, 0:128] = diag
    dst[128:256, 128:256] = diag
    dst[112:128, 128:256] = jnp.where(d < -64, ring, zero)[112:].astype(BF16)
    dst[128:144, 0:128] = jnp.where(d > 64, ring, zero)[:16].astype(BF16)


def dot(a, b):
    return jnp.dot(a, b, preferred_element_type=F32)


def stamps_kernel(group, parts, per, ids, tls, bounds, gain, weight, rows, pix, *rest):
    tin = rest[: len(parts)]
    out = rest[len(parts)]
    tiles, acc, outb, pbuf, mats, blur, resi, back, tsem, psem, osem = rest[len(parts) + 1 :]
    first = bounds[group]
    n = bounds[group + 1] - first
    steps = (n + per - 1) // per
    loads = [
        pltpu.make_async_copy(t, tiles.at[s : s + t.shape[0], r : r + t.shape[1]], tsem.at[k])
        for k, (t, (s, r)) in enumerate(zip(tin, parts))
    ]
    for c in loads:
        c.start()

    def fetch(step, slot):
        return [
            pltpu.make_async_copy(
                pix.at[ids[first + step * per + u]], pbuf.at[slot, u], psem.at[slot, u]
            )
            for u in range(per)
        ]

    @pl.when(steps > 0)
    def _():
        for c in fetch(0, 0):
            c.start()

    acc[...] = jnp.zeros_like(acc)
    mats[...] = jnp.zeros_like(mats)
    for c in loads:
        c.wait()

    def body(step, carry):
        slot = lax.rem(step, 2)

        @pl.when(step + 1 < steps)
        def _():
            for c in fetch(step + 1, 1 - slot):
                c.start()

        at = [step * per + u for u in range(per)]
        idx = [ids[first + a] for a in at]
        for u in range(per):
            for m in range(4):
                build(rows[idx[u], m : m + 1, :], mats.at[u, m])
        for c in fetch(step, slot):
            c.wait()
        t = [jnp.where(a < n, tls[first + a], 0) for a in at]
        g = [jnp.where(a < n, gain[i], 0.0) for a, i in zip(at, idx)]
        w = [weight[i] for i in idx]
        for u in range(per):
            blur[u] = dot(tiles[t[u]], mats[u, 3]).astype(BF16)
        for u in range(per):
            predicted = g[u] * dot(mats[u, 0], blur[u])
            resi[u] = (w[u] * (predicted - pbuf[slot, u].astype(F32))).astype(BF16)
        for u in range(per):
            back[u] = dot(mats[u, 1], resi[u]).astype(BF16)
        for u in range(per):
            acc[t[u]] += g[u] * dot(back[u], mats[u, 2])
        return carry

    lax.fori_loop(0, steps, body, 0)

    @pl.loop(0, acc.shape[0])
    def _(k):
        outb[k] = acc[k].astype(BF16)

    c = pltpu.make_async_copy(outb, out, osem)
    c.start()
    c.wait()


def stamps(group, units, order, gain, weight, rows, pix, per=4):
    lo, hi = GROUPS[group]
    parts, arrays = [], []
    for number in range(lo, hi):
        for array, band, row in units[UNITS[number]]:
            parts.append(((number - lo) * BANDS + band, row))
            arrays.append(array)
    n_tiles = (hi - lo) * BANDS
    smem = pl.BlockSpec(memory_space=pltpu.SMEM)
    anys = pl.BlockSpec(memory_space=pl.ANY)
    return pl.pallas_call(
        functools.partial(stamps_kernel, group, parts, per),
        out_shape=jax.ShapeDtypeStruct((n_tiles, TS, TS), BF16),
        in_specs=[smem] * 5 + [pl.BlockSpec(memory_space=pltpu.VMEM), anys] + [anys] * len(parts),
        out_specs=anys,
        scratch_shapes=[
            pltpu.VMEM((n_tiles, TS, TS), BF16),
            pltpu.VMEM((n_tiles, TS, TS), F32),
            pltpu.VMEM((n_tiles, TS, TS), BF16),
            pltpu.VMEM((2, per, TS, TS), BF16),
            pltpu.VMEM((per, 4, TS, TS), BF16),
            pltpu.VMEM((per, TS, TS), BF16),
            pltpu.VMEM((per, TS, TS), BF16),
            pltpu.VMEM((per, TS, TS), BF16),
            pltpu.SemaphoreType.DMA((len(parts),)),
            pltpu.SemaphoreType.DMA((2, per)),
            pltpu.SemaphoreType.DMA,
        ],
        compiler_params=pltpu.CompilerParams(vmem_limit_bytes=48 * 2**20),
        cost_estimate=pl.CostEstimate(
            flops=8 * TS**3 * 43 * 2, bytes_accessed=16 * 2**20, transcendentals=0
        ),
        name=f"stamps{group}",
    )(*order, gain, weight, rows, pix, *arrays)


def add_into(dst, d0, src, s0, count):
    @pl.loop(0, count)
    def _(k):
        dst[d0 + k] = (dst[d0 + k].astype(F32) + src[s0 + k].astype(F32)).astype(BF16)


def reduce_kernel(g0, g1, g2, sky, out, sq, own, quarter, diag, three, two, one,
                  skyb, lsem, ssem, rsem):
    barrier = pltpu.get_barrier_semaphore()
    for link in LINKS:
        pl.semaphore_signal(
            barrier, inc=1, device_id={"patch": neighbour(link)}, device_id_type=MESH
        )
    loads = [
        pltpu.make_async_copy(g, own.at[lo * BANDS : hi * BANDS], lsem.at[k])
        for k, (g, (lo, hi)) in enumerate(zip((g0, g1, g2), GROUPS))
    ]
    loads.append(pltpu.make_async_copy(sky, skyb, lsem.at[3]))
    for k in (2, 1, 0, 3):
        loads[k].start()
    pl.semaphore_wait(barrier, 4)

    def at(offset, half):
        return UNIT[offset] * BANDS + half * HALF

    def send(link, piece, src, dst):
        return pltpu.make_async_remote_copy(
            src_ref=src,
            dst_ref=dst,
            send_sem=ssem.at[link, piece],
            recv_sem=rsem.at[link, piece],
            device_id={"patch": neighbour(LINKS[link])},
            device_id_type=MESH,
        )

    copies, info = [], []
    for k, link in enumerate(LINKS):
        dz, dx = link
        late = 0 if dz + dx > 0 else 1
        early = 1 - late
        along_x = dz == 0
        far = (2, dx) if along_x else (dz, 2)
        straight = (0, 2) if along_x else (2, 0)
        sides = [(s, dx) if along_x else (dz, s) for s in (1, -1)]
        diag_half = 1 if along_x else 0
        row = [send(k, 0, own.at[at((2, 2), 0) : at((2, 2), 0) + BANDS, k * 64 : k * 64 + 64], quarter.at[k])]

        def half(piece, offset, h, dst):
            return send(k, piece, own.at[at(offset, h) : at(offset, h) + HALF], dst)

        row.append(half(1, sides[0], diag_half, diag.at[k, 0:HALF]))
        row.append(half(2, far, 0, three.at[k, 0:HALF]))
        row.append(half(3, far, 1, three.at[k, HALF:BANDS]))
        row.append(half(4, sides[1], diag_half, diag.at[k, HALF:BANDS]))
        row.append(half(5, straight, late, two.at[k]))
        row.append(half(6, link, early, one.at[k, early * HALF : early * HALF + HALF]))
        row.append(half(7, link, late, one.at[k, late * HALF : late * HALF + HALF]))
        copies.append(row)
        info.append((far, straight, sides, diag_half, early, late))

    loads[2].wait()
    for k in range(4):
        copies[k][0].start()
    loads[1].wait()
    for k in range(4):
        copies[k][1].start()
    for k in range(4):
        copies[k][0].wait_recv()
        far = info[k][0]

        @pl.loop(0, BANDS)
        def _(b):
            t = at(far, 0) + b
            r = slice(k * 64, k * 64 + 64)
            own[t, r] = (own[t, r].astype(F32) + quarter[k, b].astype(F32)).astype(BF16)

        copies[k][2].start()
        copies[k][3].start()
        copies[k][4].start()
    for h in range(2):
        for k in range(4):
            copies[k][2 + h].wait_recv()
            target = (2, 0) if LINKS[k][0] == 0 else (0, 2)
            add_into(own, at(target, h), three.at[k], h * HALF, HALF)
        for k in range(4):
            if info[k][5] == h:
                copies[k][5].start()
    loads[0].wait()
    for k in range(4):
        sides, diag_half = info[k][2:4]
        for s in range(2):
            copies[k][1 if s == 0 else 4].wait_recv()
            dz, dx = sides[s]
            target = (dz, 0) if LINKS[k][0] == 0 else (0, dx)
            add_into(own, at(target, diag_half), diag.at[k], s * HALF, HALF)
    for k in range(4):
        copies[k][6].start()
    for k in range(4):
        copies[k][5].wait_recv()
        add_into(own, at(LINKS[k], info[k][5]), two.at[k], 0, HALF)
        copies[k][7].start()
    loads[3].wait()
    for k in range(4):
        copies[k][6].wait_recv()
        copies[k][7].wait_recv()

    def finish(b, total):
        gradient = own[b].astype(F32)
        for k in range(4):
            gradient = gradient + one[k, b].astype(F32)
        step_field = STEP_RATE * gradient
        skyb[b] = skyb[b] - step_field
        squares = (step_field * step_field).reshape(TS // 8, 8, TS).sum(0)
        return total + squares[:, :128] + squares[:, 128:]

    sq[...] = lax.fori_loop(0, BANDS, finish, jnp.zeros((8, 128), F32))
    c = pltpu.make_async_copy(skyb, out, lsem.at[3])
    c.start()
    for k in range(4):
        for c2 in copies[k]:
            c2.wait_send()
    c.wait()


def reduce_tiles(g0, g1, g2, sky):
    anys = pl.BlockSpec(memory_space=pl.ANY)
    return pl.pallas_call(
        reduce_kernel,
        out_shape=(
            jax.ShapeDtypeStruct((BANDS, TS, TS), F32),
            jax.ShapeDtypeStruct((8, 128), F32),
        ),
        in_specs=[anys] * 4,
        out_specs=(anys, pl.BlockSpec(memory_space=pltpu.VMEM)),
        scratch_shapes=[
            pltpu.VMEM((16 * BANDS, TS, TS), BF16),
            pltpu.VMEM((4, BANDS, 64, TS), BF16),
            pltpu.VMEM((4, BANDS, TS, TS), BF16),
            pltpu.VMEM((4, BANDS, TS, TS), BF16),
            pltpu.VMEM((4, HALF, TS, TS), BF16),
            pltpu.VMEM((4, BANDS, TS, TS), BF16),
            pltpu.VMEM((BANDS, TS, TS), F32),
            pltpu.SemaphoreType.DMA((4,)),
            pltpu.SemaphoreType.DMA((4, 8)),
            pltpu.SemaphoreType.DMA((4, 8)),
        ],
        compiler_params=pltpu.CompilerParams(
            collective_id=1, has_side_effects=True, vmem_limit_bytes=48 * 2**20
        ),
        name="reduce_tiles",
    )(g0, g1, g2, sky)


def total_kernel(sq, out, held, sums, ssem, rsem, ssem2, rsem2):
    patch, exp = lax.axis_index("patch"), lax.axis_index("exp")
    barrier = pltpu.get_barrier_semaphore()
    peers = [("patch", lax.rem(patch + k, 16)) for k in range(1, 16)]
    peers += [("exp", lax.rem(exp + k, 8)) for k in range(1, 8)]
    for peer in peers:
        pl.semaphore_signal(barrier, inc=1, device_id=dict([peer]), device_id_type=MESH)
    pl.semaphore_wait(barrier, len(peers))
    held[patch] = sq[...]
    first = [
        pltpu.make_async_remote_copy(
            src_ref=sq, dst_ref=held.at[patch], send_sem=ssem.at[k], recv_sem=rsem.at[k],
            device_id=dict([peer]), device_id_type=MESH,
        )
        for k, peer in enumerate(peers[:15])
    ]
    for c in first:
        c.start()
    for c in first:
        c.wait()
    sums[exp] = jnp.sum(held[...], 0)
    second = [
        pltpu.make_async_remote_copy(
            src_ref=sums.at[exp], dst_ref=sums.at[exp], send_sem=ssem2.at[k], recv_sem=rsem2.at[k],
            device_id=dict([peer]), device_id_type=MESH,
        )
        for k, peer in enumerate(peers[15:])
    ]
    for c in second:
        c.start()
    for c in second:
        c.wait()
    out[...] = jnp.sum(sums[...], 0)


def total_of(sq):
    vmem = pl.BlockSpec(memory_space=pltpu.VMEM)
    return pl.pallas_call(
        total_kernel,
        out_shape=jax.ShapeDtypeStruct((8, 128), F32),
        in_specs=[vmem],
        out_specs=vmem,
        scratch_shapes=[
            pltpu.VMEM((16, 8, 128), F32),
            pltpu.VMEM((8, 8, 128), F32),
            pltpu.SemaphoreType.DMA((15,)),
            pltpu.SemaphoreType.DMA((15,)),
            pltpu.SemaphoreType.DMA((7,)),
            pltpu.SemaphoreType.DMA((7,)),
        ],
        compiler_params=pltpu.CompilerParams(collective_id=2, has_side_effects=True),
        name="total",
    )(sq)


def per_device(
    sky_model, stamp_pixels, stamp_patch, stamp_band, psf_taps, stamp_gain, stamp_weight
):
    sky = sky_model.reshape(BANDS, TS, TS)
    model_half = sky.astype(BF16)
    units = gather_units(model_half[:HALF], model_half[HALF:])
    order = stamp_order(stamp_patch[:, 0], stamp_band)
    rows = tap_rows(psf_taps)
    gain, weight = stamp_gain.astype(F32), stamp_weight.astype(F32)
    sums = [stamps(k, units, order, gain, weight, rows, stamp_pixels) for k in range(3)]
    new_model, squares = reduce_tiles(*sums, sky)
    square_sum = jnp.sum(total_of(squares))
    entry_count = lax.axis_size("patch") * lax.axis_size("exp") * BANDS * TS * TS
    step_rms = jnp.sqrt(square_sum / entry_count + 1e-06)
    return (new_model.reshape(sky_model.shape), step_rms)


def solution(mesh):
    return jax.shard_map(
        per_device,
        mesh=mesh,
        in_specs=(
            P("patch", "exp", None, None, None),
            P(("patch", "exp"), None, None),
            P(("patch", "exp"), None),
            P(("patch", "exp")),
            P(("patch", "exp"), None, None),
            P(("patch", "exp")),
            P(("patch", "exp")),
        ),
        out_specs=(P("patch", "exp", None, None, None), P()),
        check_vma=False,
    )
```

time: 559 us -> 239 us (0.43)
  Pallas kernels: 0 us -> 145 us
  waiting for transfers between devices: 185 us -> 44.7 us
  matrix products: 119 us -> 0 us
  other arithmetic: 95.3 us -> 3.57 us
  local copies, waits for them, and re-layouts: 77 us -> 3.12 us
  blocking collectives: 64.5 us -> 0 us
  starting transfers between devices: 0.08 us -> 39.5 us
  between operations: 15.9 us -> 2.89 us
    pallas_call x0 -> x5, Pallas kernels: none -> 145 us  [the longest x1 64.7 us: reduce_tiles(): pl.pallas_call(reduce_kernel, out_shape=(jax.ShapeDtypeStruct((BANDS, TS,...]
    dot_general x20 -> x0, matrix products: 119 us -> none  [the longest x4 42.6 us: stamp_adjoint(): jnp.einsum('sba,sbc->sac', row_kernel, residual, preferred_element_type=j...]
    unnamed x3 -> x0, waiting for transfers between devices: 94 us -> none
    all_gather x1 -> x0, waiting for transfers between devices: 91.4 us -> none  [per_device(): gathered = lax.all_gather(model_half, 'patch', axis=0, tiled=True)]
    scatter-add x4 -> x0, other arithmetic: 75.6 us -> none  [source_block(): return (running.at[keys_block].add(adjoint), None)]
    psum x1 -> x0, blocking collectives: 64.5 us -> none  [per_device(): square_sum = lax.psum(jnp.sum(step_field * step_field), ('patch', 'exp'))]
    ppermute x0 -> x32, waiting for transfers between devices: none -> 44.7 us  [from_offset(): return lax.ppermute(value, 'patch', pairs)]
    ppermute x0 -> x32, starting transfers between devices: none -> 39.5 us  [from_offset(): return lax.ppermute(value, 'patch', pairs)]
  transfers between devices with their start and end apart: 2 -> 32, of which waited for: 2 -> 10; matrix products, arithmetic and copies ran while one was open for 1% -> 1% of each run, Pallas kernels for 0% -> 16%
where the time goes in v1:
time: 239 us
  Pallas kernels  145 us (61%)
  waiting for transfers between devices  44.7 us (19%)
  starting transfers between devices  39.5 us (17%)
  other arithmetic  3.57 us (1%)
  local copies, waits for them, and re-layouts  3.12 us (1%)
  between operations  2.89 us (1%)
    pallas_call x1, Pallas kernels, reduce_tiles(): pl.pallas_call(reduce_kernel, out_shape=(jax.ShapeDtypeStruct((BANDS, TS,...  64.7 us
    pallas_call x3, Pallas kernels, stamps(): pl.pallas_call(functools.partial(stamps_kernel, group, parts, per), out_s...  56.1 us
    ppermute x32, waiting for transfers between devices, from_offset(): return lax.ppermute(value, 'patch', pairs)  44.7 us
    ppermute x32, starting transfers between devices, from_offset(): return lax.ppermute(value, 'patch', pairs)  39.5 us
    pallas_call x1, Pallas kernels, total_of(): pl.pallas_call(total_kernel, out_shape=jax.ShapeDtypeStruct((8, 128), F32...  24.2 us
  transfers between devices with their start and end apart: 32, of which 10 were waited for; matrix products, arithmetic and copies ran while one was open for 1% of the time, Pallas kernels for 16%

profile of v1, /device:TPU:1, one launch (start us, length us, event | category | flops | bytes accessed | tf_op | source)
XLA Modules:
  0.0 238.8 jit_solution(9183536141060964445)
XLA Ops:
  0.7 1.5 bitcast_convert_fusion
  2.3 2.5 %collective-permute-start.7 = (bf16[3,256,256]{2,1,0:T(8,128)(2,1)S(1)}, bf16[3,256,256]{2,1,0:T(8,128)(2,1)S(1)}, u32[]{:S(2)}, u32[]{:S(2)}) collective-permute-start(bf16[3,256,256]{2,1,0:T(8,128)(2,1)S(1)} %get-tuple-element.10.rest_1_), channel_id=1, source_target_pairs={{96,0},{104,8},{112,16},{120,24},{0,32},{8,40},{16,48},{24,56},{32... | collective-permute-start | bytes 1179656 | tf_op jit(solution)/shard_map/ppermute | solution.py:43
  4.8 2.2 collective-permute-start.5
  8.2 1.5 collective-permute-start.1
  10.8 4.9 %collective-permute-done.7.rest_9_ = bf16[3,256,256]{2,1,0:T(8,128)(2,1)S(1)} collective-permute-done((bf16[3,256,256]{2,1,0:T(8,128)(2,1)S(1)}, bf16[3,256,256]{2,1,0:T(8,128)(2,1)S(1)}, u32[]{:S(2)}, u32[]{:S(2)}) %collective-permute-start.7) | collective-permute-done | bytes 393248 | tf_op jit(solution)/shard_map/ppermute | solution.py:43
  18.1 1.5 collective-permute-start
  19.8 4.4 %collective-permute-done.6.rest_8_ = bf16[3,256,256]{2,1,0:T(8,128)(2,1)S(1)} collective-permute-done((bf16[3,256,256]{2,1,0:T(8,128)(2,1)S(1)}, bf16[3,256,256]{2,1,0:T(8,128)(2,1)S(1)}, u32[]{:S(2)}, u32[]{:S(2)}) %collective-permute-start.6) | collective-permute-done | bytes 393248 | tf_op jit(solution)/shard_map/ppermute | solution.py:43
  24.2 2.5 %collective-permute-start.17 = (bf16[3,256,256]{2,1,0:T(8,128)(2,1)S(1)}, bf16[3,256,256]{2,1,0:T(8,128)(2,1)S(1)}, u32[]{:S(2)}, u32[]{:S(2)}) collective-permute-start(bf16[3,256,256]{2,1,0:T(8,128)(2,1)S(1)} %collective-permute-done.7.rest_9_), channel_id=1, source_target_pairs={{8,0},{16,8},{24,16},{0,24},{40,32},{48,40},{56,48},{32,56},{72,64... | collective-permute-start | bytes 1179656 | tf_op jit(solution)/shard_map/ppermute | solution.py:43
  26.8 2.7 %collective-permute-start.10 = (bf16[3,256,256]{2,1,0:T(8,128)(2,1)S(1)}, bf16[3,256,256]{2,1,0:T(8,128)(2,1)S(1)}, u32[]{:S(2)}, u32[]{:S(2)}) collective-permute-start(bf16[3,256,256]{2,1,0:T(8,128)(2,1)S(1)} %collective-permute-done.4.rest_6_), channel_id=1, source_target_pairs={{32,0},{40,8},{48,16},{56,24},{64,32},{72,40},{80,48},{88,56},{96,... | collective-permute-start | bytes 1179656 | tf_op jit(solution)/shard_map/ppermute | solution.py:43
  29.5 4.7 %collective-permute-done.19.rest_11_ = bf16[3,256,256]{2,1,0:T(8,128)(2,1)S(1)} collective-permute-done((bf16[3,256,256]{2,1,0:T(8,128)(2,1)S(1)}, bf16[3,256,256]{2,1,0:T(8,128)(2,1)S(1)}, u32[]{:S(2)}, u32[]{:S(2)}) %collective-permute-start.19) | collective-permute-done | bytes 393248 | tf_op jit(solution)/shard_map/ppermute | solution.py:43
  34.2 1.5 collective-permute-done.17.rest_9_
  35.7 3.4 %collective-permute-start.8 = (bf16[3,256,256]{2,1,0:T(8,128)(2,1)S(1)}, bf16[3,256,256]{2,1,0:T(8,128)(2,1)S(1)}, u32[]{:S(2)}, u32[]{:S(2)}) collective-permute-start(bf16[3,256,256]{2,1,0:T(8,128)(2,1)S(1)} %collective-permute-done.rest_2_), channel_id=1, source_target_pairs={{8,0},{16,8},{24,16},{0,24},{40,32},{48,40},{56,48},{32,56},{72,64... | collective-permute-start | bytes 1179656 | tf_op jit(solution)/shard_map/ppermute | solution.py:43
  39.1 3.5 %collective-permute-done.15.rest_7_ = bf16[3,256,256]{2,1,0:T(8,128)(2,1)S(1)} collective-permute-done((bf16[3,256,256]{2,1,0:T(8,128)(2,1)S(1)}, bf16[3,256,256]{2,1,0:T(8,128)(2,1)S(1)}, u32[]{:S(2)}, u32[]{:S(2)}) %collective-permute-start.15) | collective-permute-done | bytes 393248 | tf_op jit(solution)/shard_map/ppermute | solution.py:43
  42.6 1.3 collective-permute-start.21
  44.8 6.3 %collective-permute-done.9.rest_1_ = bf16[3,256,256]{2,1,0:T(8,128)(2,1)S(1)} collective-permute-done((bf16[3,256,256]{2,1,0:T(8,128)(2,1)S(1)}, bf16[3,256,256]{2,1,0:T(8,128)(2,1)S(1)}, u32[]{:S(2)}, u32[]{:S(2)}) %collective-permute-start.9) | collective-permute-done | bytes 393248 | tf_op jit(solution)/shard_map/ppermute | solution.py:43
  52.0 1.7 collective-permute-start.25
  53.7 5.7 %collective-permute-done.23.rest_3_ = bf16[3,256,256]{2,1,0:T(8,128)(2,1)S(1)} collective-permute-done((bf16[3,256,256]{2,1,0:T(8,128)(2,1)S(1)}, bf16[3,256,256]{2,1,0:T(8,128)(2,1)S(1)}, u32[]{:S(2)}, u32[]{:S(2)}) %collective-permute-start.23) | collective-permute-done | bytes 393248 | tf_op jit(solution)/shard_map/ppermute | solution.py:43
  59.5 1.3 collective-permute-start.20
  61.7 6.2 %collective-permute-done.22.rest_2_ = bf16[3,256,256]{2,1,0:T(8,128)(2,1)S(1)} collective-permute-done((bf16[3,256,256]{2,1,0:T(8,128)(2,1)S(1)}, bf16[3,256,256]{2,1,0:T(8,128)(2,1)S(1)}, u32[]{:S(2)}, u32[]{:S(2)}) %collective-permute-start.22) | collective-permute-done | bytes 393248 | tf_op jit(solution)/shard_map/ppermute | solution.py:43
  67.9 2.5 %collective-permute-start.24 = (bf16[3,256,256]{2,1,0:T(8,128)(2,1)S(1)}, bf16[3,256,256]{2,1,0:T(8,128)(2,1)S(1)}, u32[]{:S(2)}, u32[]{:S(2)}) collective-permute-start(bf16[3,256,256]{2,1,0:T(8,128)(2,1)S(1)} %collective-permute-done.8.rest_0_), channel_id=1, source_target_pairs={{32,0},{40,8},{48,16},{56,24},{64,32},{72,40},{80,48},{88,56},{96,... | collective-permute-start | bytes 1179656 | tf_op jit(solution)/shard_map/ppermute | solution.py:43
  70.3 17.4 %stamps0.1.g0 = bf16[30,256,256]{2,1,0:T(8,128)(2,1)} custom-call(s32[136]{0:T(256)S(1)} %get-tuple-element.7.ids, s32[136]{0:T(256)S(1)} %get-tuple-element.6.tls, s32[4]{0:T(128)S(1)} %convert_reduce_fusion.1.bounds, f32[128]{0:T(128)S(1)} %convert_element_type.53.gain, f32[128]{0:T(128)S(1)} %convert_element_type.54.weight, ...), custom_call_target="tpu_custom_call" | custom-call | flops 11542724608 | bytes 16777216 | tf_op jit(solution)/shard_map/stamps0/pallas_call | solution.py:210
  87.8 1.5 collective-permute-start.13
  89.5 2.5 %collective-permute-start.14 = (bf16[3,256,256]{2,1,0:T(8,128)(2,1)S(1)}, bf16[3,256,256]{2,1,0:T(8,128)(2,1)S(1)}, u32[]{:S(2)}, u32[]{:S(2)}) collective-permute-start(bf16[3,256,256]{2,1,0:T(8,128)(2,1)S(1)} %collective-permute-done.2.rest_4_), channel_id=1, source_target_pairs={{32,0},{40,8},{48,16},{56,24},{64,32},{72,40},{80,48},{88,56},{96,... | collective-permute-start | bytes 1179656 | tf_op jit(solution)/shard_map/ppermute | solution.py:43
  92.0 2.7 %collective-permute-start.12 = (bf16[3,256,256]{2,1,0:T(8,128)(2,1)S(1)}, bf16[3,256,256]{2,1,0:T(8,128)(2,1)S(1)}, u32[]{:S(2)}, u32[]{:S(2)}) collective-permute-start(bf16[3,256,256]{2,1,0:T(8,128)(2,1)S(1)} %collective-permute-done.rest_2_), channel_id=1, source_target_pairs={{32,0},{40,8},{48,16},{56,24},{64,32},{72,40},{80,48},{88,56},{96,... | collective-permute-start | bytes 1179656 | tf_op jit(solution)/shard_map/ppermute | solution.py:43
  94.9 1.9 collective-permute-done.13.rest_5_
  97.9 2.7 %collective-permute-start.28 = (bf16[6,64,256]{2,1,0:T(8,128)(2,1)S(1)}, bf16[6,64,256]{2,1,0:T(8,128)(2,1)S(1)}, u32[]{:S(2)}, u32[]{:S(2)}) collective-permute-start(bf16[6,64,256]{2,1,0:T(8,128)(2,1)S(1)} %pad_maximum_fusion), channel_id=1, source_target_pairs={{8,0},{16,8},{24,16},{0,24},{40,32},{48,40},{56,48},{32,56},{72,64... | collective-permute-start | bytes 589832 | tf_op jit(solution)/shard_map/ppermute | solution.py:43
  100.7 5.6 %collective-permute-done.16.rest_8_ = bf16[3,256,256]{2,1,0:T(8,128)(2,1)S(1)} collective-permute-done((bf16[3,256,256]{2,1,0:T(8,128)(2,1)S(1)}, bf16[3,256,256]{2,1,0:T(8,128)(2,1)S(1)}, u32[]{:S(2)}, u32[]{:S(2)}) %collective-permute-start.16) | collective-permute-done | bytes 393248 | tf_op jit(solution)/shard_map/ppermute | solution.py:43
  106.3 20.4 %stamps1.1.g1 = bf16[36,256,256]{2,1,0:T(8,128)(2,1)} custom-call(s32[136]{0:T(256)S(1)} %get-tuple-element.7.ids, s32[136]{0:T(256)S(1)} %get-tuple-element.6.tls, s32[4]{0:T(128)S(1)} %convert_reduce_fusion.1.bounds, f32[128]{0:T(128)S(1)} %convert_element_type.53.gain, f32[128]{0:T(128)S(1)} %convert_element_type.54.weight, ...), custom_call_target="tpu_custom_call" | custom-call | flops 11542724608 | bytes 16777216 | tf_op jit(solution)/shard_map/stamps1/pallas_call | solution.py:210
  126.7 18.3 %stamps2.1.g2 = bf16[30,256,256]{2,1,0:T(8,128)(2,1)} custom-call(s32[136]{0:T(256)S(1)} %get-tuple-element.7.ids, s32[136]{0:T(256)S(1)} %get-tuple-element.6.tls, s32[4]{0:T(128)S(1)} %convert_reduce_fusion.1.bounds, f32[128]{0:T(128)S(1)} %convert_element_type.53.gain, f32[128]{0:T(128)S(1)} %convert_element_type.54.weight, ...), custom_call_target="tpu_custom_call" | custom-call | flops 11542724608 | bytes 16777216 | tf_op jit(solution)/shard_map/stamps2/pallas_call | solution.py:210
  145.1 64.7 %reduce_tiles.1 = (f32[6,256,256]{2,1,0:T(8,128)S(1)}, f32[8,128]{1,0:T(8,128)S(1)}) custom-call(bf16[30,256,256]{2,1,0:T(8,128)(2,1)} %stamps0.1.g0, bf16[36,256,256]{2,1,0:T(8,128)(2,1)} %stamps1.1.g1, bf16[30,256,256]{2,1,0:T(8,128)(2,1)} %stamps2.1.g2, f32[6,256,256]{2,1,0:T(8,128)S(1)} %bitcast.26), custom_call_target="tpu_custom_call" | custom-call | tf_op jit(solution)/shard_map/reduce_tiles/pallas_call | solution.py:362
  210.4 24.2 %total.1 = f32[8,128]{1,0:T(8,128)} custom-call(f32[8,128]{1,0:T(8,128)} %copy-done.1), custom_call_target="tpu_custom_call" | custom-call | tf_op jit(solution)/shard_map/total/pallas_call | solution.py:426
  234.6 1.3 reduce_sum.49
  (89 shorter events, 11.1 us)
Async XLA Ops:
  2.3 13.5 %collective-permute-start.7 = (bf16[3,256,256]{2,1,0:T(8,128)(2,1)S(1)}, bf16[3,256,256]{2,1,0:T(8,128)(2,1)S(1)}, u32[]{:S(2)}, u32[]{:S(2)}) collective-permute-start(bf16[3,256,256]{2,1,0:T(8,128)(2,1)S(1)} %get-tuple-element.10.rest_1_), channel_id=1, source_target_pairs={{96,0},{104,8},{112,16},{120,24},{0,32},{8,40},{16,48},{24,56},{32... | collective-permute-start | bytes 1179656 | tf_op jit(solution)/shard_map/ppermute | solution.py:43
  4.8 12.1 %collective-permute-start.5 = (bf16[3,256,256]{2,1,0:T(8,128)(2,1)S(1)}, bf16[3,256,256]{2,1,0:T(8,128)(2,1)S(1)}, u32[]{:S(2)}, u32[]{:S(2)}) collective-permute-start(bf16[3,256,256]{2,1,0:T(8,128)(2,1)S(1)} %get-tuple-element.10.rest_1_), channel_id=1, source_target_pairs={{32,0},{40,8},{48,16},{56,24},{64,32},{72,40},{80,48},{88,56},{96,... | collective-permute-start | bytes 1179656 | tf_op jit(solution)/shard_map/ppermute | solution.py:43
  7.0 11.1 %collective-permute-start.3 = (bf16[3,256,256]{2,1,0:T(8,128)(2,1)S(1)}, bf16[3,256,256]{2,1,0:T(8,128)(2,1)S(1)}, u32[]{:S(2)}, u32[]{:S(2)}) collective-permute-start(bf16[3,256,256]{2,1,0:T(8,128)(2,1)S(1)} %get-tuple-element.10.rest_1_), channel_id=1, source_target_pairs={{24,0},{0,8},{8,16},{16,24},{56,32},{32,40},{40,48},{48,56},{88,64... | collective-permute-start | bytes 1179656 | tf_op jit(solution)/shard_map/ppermute | solution.py:43
  8.2 11.5 %collective-permute-start.1 = (bf16[3,256,256]{2,1,0:T(8,128)(2,1)S(1)}, bf16[3,256,256]{2,1,0:T(8,128)(2,1)S(1)}, u32[]{:S(2)}, u32[]{:S(2)}) collective-permute-start(bf16[3,256,256]{2,1,0:T(8,128)(2,1)S(1)} %get-tuple-element.10.rest_1_), channel_id=1, source_target_pairs={{8,0},{16,8},{24,16},{0,24},{40,32},{48,40},{56,48},{32,56},{72,64... | collective-permute-start | bytes 1179656 | tf_op jit(solution)/shard_map/ppermute | solution.py:43
  9.7 14.5 %collective-permute-start.6 = (bf16[3,256,256]{2,1,0:T(8,128)(2,1)S(1)}, bf16[3,256,256]{2,1,0:T(8,128)(2,1)S(1)}, u32[]{:S(2)}, u32[]{:S(2)}) collective-permute-start(bf16[3,256,256]{2,1,0:T(8,128)(2,1)S(1)} %get-tuple-element.11.rest_0_), channel_id=1, source_target_pairs={{96,0},{104,8},{112,16},{120,24},{0,32},{8,40},{16,48},{24,56},{32... | collective-permute-start | bytes 1179656 | tf_op jit(solution)/shard_map/ppermute | solution.py:43
  15.8 10.9 %collective-permute-start.4 = (bf16[3,256,256]{2,1,0:T(8,128)(2,1)S(1)}, bf16[3,256,256]{2,1,0:T(8,128)(2,1)S(1)}, u32[]{:S(2)}, u32[]{:S(2)}) collective-permute-start(bf16[3,256,256]{2,1,0:T(8,128)(2,1)S(1)} %get-tuple-element.11.rest_0_), channel_id=1, source_target_pairs={{32,0},{40,8},{48,16},{56,24},{64,32},{72,40},{80,48},{88,56},{96,... | collective-permute-start | bytes 1179656 | tf_op jit(solution)/shard_map/ppermute | solution.py:43
  16.9 9.8 %collective-permute-start.2 = (bf16[3,256,256]{2,1,0:T(8,128)(2,1)S(1)}, bf16[3,256,256]{2,1,0:T(8,128)(2,1)S(1)}, u32[]{:S(2)}, u32[]{:S(2)}) collective-permute-start(bf16[3,256,256]{2,1,0:T(8,128)(2,1)S(1)} %get-tuple-element.11.rest_0_), channel_id=1, source_target_pairs={{24,0},{0,8},{8,16},{16,24},{56,32},{32,40},{40,48},{48,56},{88,64... | collective-permute-start | bytes 1179656 | tf_op jit(solution)/shard_map/ppermute | solution.py:43
  18.1 8.6 %collective-permute-start = (bf16[3,256,256]{2,1,0:T(8,128)(2,1)S(1)}, bf16[3,256,256]{2,1,0:T(8,128)(2,1)S(1)}, u32[]{:S(2)}, u32[]{:S(2)}) collective-permute-start(bf16[3,256,256]{2,1,0:T(8,128)(2,1)S(1)} %get-tuple-element.11.rest_0_), channel_id=1, source_target_pairs={{8,0},{16,8},{24,16},{0,24},{40,32},{48,40},{56,48},{32,56},{72,64... | collective-permute-start | bytes 1179656 | tf_op jit(solution)/shard_map/ppermute | solution.py:43
  19.7 14.4 %collective-permute-start.19 = (bf16[3,256,256]{2,1,0:T(8,128)(2,1)S(1)}, bf16[3,256,256]{2,1,0:T(8,128)(2,1)S(1)}, u32[]{:S(2)}, u32[]{:S(2)}) collective-permute-start(bf16[3,256,256]{2,1,0:T(8,128)(2,1)S(1)} %collective-permute-done.7.rest_9_), channel_id=1, source_target_pairs={{24,0},{0,8},{8,16},{16,24},{56,32},{32,40},{40,48},{48,56},{88,64... | collective-permute-start | bytes 1179656 | tf_op jit(solution)/shard_map/ppermute | solution.py:43
  24.2 11.5 %collective-permute-start.17 = (bf16[3,256,256]{2,1,0:T(8,128)(2,1)S(1)}, bf16[3,256,256]{2,1,0:T(8,128)(2,1)S(1)}, u32[]{:S(2)}, u32[]{:S(2)}) collective-permute-start(bf16[3,256,256]{2,1,0:T(8,128)(2,1)S(1)} %collective-permute-done.7.rest_9_), channel_id=1, source_target_pairs={{8,0},{16,8},{24,16},{0,24},{40,32},{48,40},{56,48},{32,56},{72,64... | collective-permute-start | bytes 1179656 | tf_op jit(solution)/shard_map/ppermute | solution.py:43
  26.7 12.4 %collective-permute-start.11 = (bf16[3,256,256]{2,1,0:T(8,128)(2,1)S(1)}, bf16[3,256,256]{2,1,0:T(8,128)(2,1)S(1)}, u32[]{:S(2)}, u32[]{:S(2)}) collective-permute-start(bf16[3,256,256]{2,1,0:T(8,128)(2,1)S(1)} %collective-permute-done.7.rest_9_), channel_id=1, source_target_pairs={{96,0},{104,8},{112,16},{120,24},{0,32},{8,40},{16,48},{24,56},{32... | collective-permute-start | bytes 1179656 | tf_op jit(solution)/shard_map/ppermute | solution.py:43
  26.7 15.9 %collective-permute-start.15 = (bf16[3,256,256]{2,1,0:T(8,128)(2,1)S(1)}, bf16[3,256,256]{2,1,0:T(8,128)(2,1)S(1)}, u32[]{:S(2)}, u32[]{:S(2)}) collective-permute-start(bf16[3,256,256]{2,1,0:T(8,128)(2,1)S(1)} %collective-permute-done.5.rest_7_), channel_id=1, source_target_pairs={{24,0},{0,8},{8,16},{16,24},{56,32},{32,40},{40,48},{48,56},{88,64... | collective-permute-start | bytes 1179656 | tf_op jit(solution)/shard_map/ppermute | solution.py:43
  26.8 17.1 %collective-permute-start.10 = (bf16[3,256,256]{2,1,0:T(8,128)(2,1)S(1)}, bf16[3,256,256]{2,1,0:T(8,128)(2,1)S(1)}, u32[]{:S(2)}, u32[]{:S(2)}) collective-permute-start(bf16[3,256,256]{2,1,0:T(8,128)(2,1)S(1)} %collective-permute-done.4.rest_6_), channel_id=1, source_target_pairs={{32,0},{40,8},{48,16},{56,24},{64,32},{72,40},{80,48},{88,56},{96,... | collective-permute-start | bytes 1179656 | tf_op jit(solution)/shard_map/ppermute | solution.py:43
  34.2 16.9 %collective-permute-start.9 = (bf16[3,256,256]{2,1,0:T(8,128)(2,1)S(1)}, bf16[3,256,256]{2,1,0:T(8,128)(2,1)S(1)}, u32[]{:S(2)}, u32[]{:S(2)}) collective-permute-start(bf16[3,256,256]{2,1,0:T(8,128)(2,1)S(1)} %collective-permute-done.3.rest_5_), channel_id=1, source_target_pairs={{24,0},{0,8},{8,16},{16,24},{56,32},{32,40},{40,48},{48,56},{88,64... | collective-permute-start | bytes 1179656 | tf_op jit(solution)/shard_map/ppermute | solution.py:43
  35.7 16.3 %collective-permute-start.8 = (bf16[3,256,256]{2,1,0:T(8,128)(2,1)S(1)}, bf16[3,256,256]{2,1,0:T(8,128)(2,1)S(1)}, u32[]{:S(2)}, u32[]{:S(2)}) collective-permute-start(bf16[3,256,256]{2,1,0:T(8,128)(2,1)S(1)} %collective-permute-done.rest_2_), channel_id=1, source_target_pairs={{8,0},{16,8},{24,16},{0,24},{40,32},{48,40},{56,48},{32,56},{72,64... | collective-permute-start | bytes 1179656 | tf_op jit(solution)/shard_map/ppermute | solution.py:43
  39.1 20.4 %collective-permute-start.23 = (bf16[3,256,256]{2,1,0:T(8,128)(2,1)S(1)}, bf16[3,256,256]{2,1,0:T(8,128)(2,1)S(1)}, u32[]{:S(2)}, u32[]{:S(2)}) collective-permute-start(bf16[3,256,256]{2,1,0:T(8,128)(2,1)S(1)} %collective-permute-done.11.rest_3_), channel_id=1, source_target_pairs={{24,0},{0,8},{8,16},{16,24},{56,32},{32,40},{40,48},{48,56},{88,64... | collective-permute-start | bytes 1179656 | tf_op jit(solution)/shard_map/ppermute | solution.py:43
  42.6 18.1 %collective-permute-start.21 = (bf16[3,256,256]{2,1,0:T(8,128)(2,1)S(1)}, bf16[3,256,256]{2,1,0:T(8,128)(2,1)S(1)}, u32[]{:S(2)}, u32[]{:S(2)}) collective-permute-start(bf16[3,256,256]{2,1,0:T(8,128)(2,1)S(1)} %collective-permute-done.11.rest_3_), channel_id=1, source_target_pairs={{8,0},{16,8},{24,16},{0,24},{40,32},{48,40},{56,48},{32,56},{72,64... | collective-permute-start | bytes 1179656 | tf_op jit(solution)/shard_map/ppermute | solution.py:43
  43.9 24.0 %collective-permute-start.22 = (bf16[3,256,256]{2,1,0:T(8,128)(2,1)S(1)}, bf16[3,256,256]{2,1,0:T(8,128)(2,1)S(1)}, u32[]{:S(2)}, u32[]{:S(2)}) collective-permute-start(bf16[3,256,256]{2,1,0:T(8,128)(2,1)S(1)} %collective-permute-done.10.rest_2_), channel_id=1, source_target_pairs={{24,0},{0,8},{8,16},{16,24},{56,32},{32,40},{40,48},{48,56},{88,64... | collective-permute-start | bytes 1179656 | tf_op jit(solution)/shard_map/ppermute | solution.py:43
  51.0 36.7 %collective-permute-start.27 = (bf16[3,256,256]{2,1,0:T(8,128)(2,1)S(1)}, bf16[3,256,256]{2,1,0:T(8,128)(2,1)S(1)}, u32[]{:S(2)}, u32[]{:S(2)}) collective-permute-start(bf16[3,256,256]{2,1,0:T(8,128)(2,1)S(1)} %collective-permute-done.9.rest_1_), channel_id=1, source_target_pairs={{96,0},{104,8},{112,16},{120,24},{0,32},{8,40},{16,48},{24,56},{32... | collective-permute-start | bytes 1179656 | tf_op jit(solution)/shard_map/ppermute | solution.py:43
  52.0 37.3 %collective-permute-start.25 = (bf16[3,256,256]{2,1,0:T(8,128)(2,1)S(1)}, bf16[3,256,256]{2,1,0:T(8,128)(2,1)S(1)}, u32[]{:S(2)}, u32[]{:S(2)}) collective-permute-start(bf16[3,256,256]{2,1,0:T(8,128)(2,1)S(1)} %collective-permute-done.9.rest_1_), channel_id=1, source_target_pairs={{32,0},{40,8},{48,16},{56,24},{64,32},{72,40},{80,48},{88,56},{96,... | collective-permute-start | bytes 1179656 | tf_op jit(solution)/shard_map/ppermute | solution.py:43
  59.5 30.0 %collective-permute-start.20 = (bf16[3,256,256]{2,1,0:T(8,128)(2,1)S(1)}, bf16[3,256,256]{2,1,0:T(8,128)(2,1)S(1)}, u32[]{:S(2)}, u32[]{:S(2)}) collective-permute-start(bf16[3,256,256]{2,1,0:T(8,128)(2,1)S(1)} %collective-permute-done.10.rest_2_), channel_id=1, source_target_pairs={{8,0},{16,8},{24,16},{0,24},{40,32},{48,40},{56,48},{32,56},{72,64... | collective-permute-start | bytes 1179656 | tf_op jit(solution)/shard_map/ppermute | solution.py:43
  60.7 31.3 %collective-permute-start.26 = (bf16[3,256,256]{2,1,0:T(8,128)(2,1)S(1)}, bf16[3,256,256]{2,1,0:T(8,128)(2,1)S(1)}, u32[]{:S(2)}, u32[]{:S(2)}) collective-permute-start(bf16[3,256,256]{2,1,0:T(8,128)(2,1)S(1)} %collective-permute-done.8.rest_0_), channel_id=1, source_target_pairs={{96,0},{104,8},{112,16},{120,24},{0,32},{8,40},{16,48},{24,56},{32... | collective-permute-start | bytes 1179656 | tf_op jit(solution)/shard_map/ppermute | solution.py:43
  67.9 24.1 %collective-permute-start.24 = (bf16[3,256,256]{2,1,0:T(8,128)(2,1)S(1)}, bf16[3,256,256]{2,1,0:T(8,128)(2,1)S(1)}, u32[]{:S(2)}, u32[]{:S(2)}) collective-permute-start(bf16[3,256,256]{2,1,0:T(8,128)(2,1)S(1)} %collective-permute-done.8.rest_0_), channel_id=1, source_target_pairs={{32,0},{40,8},{48,16},{56,24},{64,32},{72,40},{80,48},{88,56},{96,... | collective-permute-start | bytes 1179656 | tf_op jit(solution)/shard_map/ppermute | solution.py:43
  87.8 9.0 %collective-permute-start.13 = (bf16[3,256,256]{2,1,0:T(8,128)(2,1)S(1)}, bf16[3,256,256]{2,1,0:T(8,128)(2,1)S(1)}, u32[]{:S(2)}, u32[]{:S(2)}) collective-permute-start(bf16[3,256,256]{2,1,0:T(8,128)(2,1)S(1)} %collective-permute-done.5.rest_7_), channel_id=1, source_target_pairs={{8,0},{16,8},{24,16},{0,24},{40,32},{48,40},{56,48},{32,56},{72,64... | collective-permute-start | bytes 1179656 | tf_op jit(solution)/shard_map/ppermute | solution.py:43
  89.3 8.6 %collective-permute-start.18 = (bf16[3,256,256]{2,1,0:T(8,128)(2,1)S(1)}, bf16[3,256,256]{2,1,0:T(8,128)(2,1)S(1)}, u32[]{:S(2)}, u32[]{:S(2)}) collective-permute-start(bf16[3,256,256]{2,1,0:T(8,128)(2,1)S(1)} %collective-permute-done.2.rest_4_), channel_id=1, source_target_pairs={{96,0},{104,8},{112,16},{120,24},{0,32},{8,40},{16,48},{24,56},{32... | collective-permute-start | bytes 1179656 | tf_op jit(solution)/shard_map/ppermute | solution.py:43
  89.5 11.2 %collective-permute-start.14 = (bf16[3,256,256]{2,1,0:T(8,128)(2,1)S(1)}, bf16[3,256,256]{2,1,0:T(8,128)(2,1)S(1)}, u32[]{:S(2)}, u32[]{:S(2)}) collective-permute-start(bf16[3,256,256]{2,1,0:T(8,128)(2,1)S(1)} %collective-permute-done.2.rest_4_), channel_id=1, source_target_pairs={{32,0},{40,8},{48,16},{56,24},{64,32},{72,40},{80,48},{88,56},{96,... | collective-permute-start | bytes 1179656 | tf_op jit(solution)/shard_map/ppermute | solution.py:43
  92.0 14.3 %collective-permute-start.16 = (bf16[3,256,256]{2,1,0:T(8,128)(2,1)S(1)}, bf16[3,256,256]{2,1,0:T(8,128)(2,1)S(1)}, u32[]{:S(2)}, u32[]{:S(2)}) collective-permute-start(bf16[3,256,256]{2,1,0:T(8,128)(2,1)S(1)} %collective-permute-done.rest_2_), channel_id=1, source_target_pairs={{96,0},{104,8},{112,16},{120,24},{0,32},{8,40},{16,48},{24,56},{32... | collective-permute-start | bytes 1179656 | tf_op jit(solution)/shard_map/ppermute | solution.py:43
  92.0 14.3 %collective-permute-start.12 = (bf16[3,256,256]{2,1,0:T(8,128)(2,1)S(1)}, bf16[3,256,256]{2,1,0:T(8,128)(2,1)S(1)}, u32[]{:S(2)}, u32[]{:S(2)}) collective-permute-start(bf16[3,256,256]{2,1,0:T(8,128)(2,1)S(1)} %collective-permute-done.rest_2_), channel_id=1, source_target_pairs={{32,0},{40,8},{48,16},{56,24},{64,32},{72,40},{80,48},{88,56},{96,... | collective-permute-start | bytes 1179656 | tf_op jit(solution)/shard_map/ppermute | solution.py:43
  96.8 29.9 %collective-permute-start.29 = (bf16[6,64,256]{2,1,0:T(8,128)(2,1)S(1)}, bf16[6,64,256]{2,1,0:T(8,128)(2,1)S(1)}, u32[]{:S(2)}, u32[]{:S(2)}) collective-permute-start(bf16[6,64,256]{2,1,0:T(8,128)(2,1)S(1)} %pad_maximum_fusion.1), channel_id=1, source_target_pairs={{24,0},{0,8},{8,16},{16,24},{56,32},{32,40},{40,48},{48,56},{88,64... | collective-permute-start | bytes 589832 | tf_op jit(solution)/shard_map/ppermute | solution.py:43
  97.9 28.7 %collective-permute-start.28 = (bf16[6,64,256]{2,1,0:T(8,128)(2,1)S(1)}, bf16[6,64,256]{2,1,0:T(8,128)(2,1)S(1)}, u32[]{:S(2)}, u32[]{:S(2)}) collective-permute-start(bf16[6,64,256]{2,1,0:T(8,128)(2,1)S(1)} %pad_maximum_fusion), channel_id=1, source_target_pairs={{8,0},{16,8},{24,16},{0,24},{40,32},{48,40},{56,48},{32,56},{72,64... | collective-permute-start | bytes 589832 | tf_op jit(solution)/shard_map/ppermute | solution.py:43
  100.7 26.0 %collective-permute-start.31 = (bf16[6,64,256]{2,1,0:T(8,128)(2,1)S(1)}, bf16[6,64,256]{2,1,0:T(8,128)(2,1)S(1)}, u32[]{:S(2)}, u32[]{:S(2)}) collective-permute-start(bf16[6,64,256]{2,1,0:T(8,128)(2,1)S(1)} %pad_maximum_fusion.3), channel_id=1, source_target_pairs={{96,0},{104,8},{112,16},{120,24},{0,32},{8,40},{16,48},{24,56},{32... | collective-permute-start | bytes 589832 | tf_op jit(solution)/shard_map/ppermute | solution.py:43
  106.2 20.4 %collective-permute-start.30 = (bf16[6,64,256]{2,1,0:T(8,128)(2,1)S(1)}, bf16[6,64,256]{2,1,0:T(8,128)(2,1)S(1)}, u32[]{:S(2)}, u32[]{:S(2)}) collective-permute-start(bf16[6,64,256]{2,1,0:T(8,128)(2,1)S(1)} %pad_maximum_fusion.2), channel_id=1, source_target_pairs={{32,0},{40,8},{48,16},{56,24},{64,32},{72,40},{80,48},{88,56},{96,... | collective-permute-start | bytes 589832 | tf_op jit(solution)/shard_map/ppermute | solution.py:43
  (7 other events, 162.9 us)

commit v2 on v0

v2 whole, which is shorter than its diff:
```python
import functools

import jax
import jax.numpy as jnp
from jax import lax
from jax.experimental import pallas as pl
from jax.experimental.pallas import tpu as pltpu
from jax.sharding import PartitionSpec as P

TS = 256
BANDS = 6
HALF = 3
STAMPS = 128
STEP_RATE = 0.2
F32, BF16 = jnp.float32, jnp.bfloat16
MESH = pl.DeviceIdType.MESH

UNITS = [
    (0, 0), (0, 1), (0, -1), (1, 0), (-1, 0),
    (0, 2), (2, 0), (1, 1), (-1, -1),
    (2, 1), (2, -1), (1, 2), (-1, 2), (1, -1), (-1, 1), (2, 2),
]
UNIT = {offset: number for number, offset in enumerate(UNITS)}
TILES = len(UNITS) * BANDS
LINKS = [(0, 1), (0, -1), (1, 0), (-1, 0)]
PER = 4


def place_on_torus():
    patch = lax.axis_index("patch")
    return patch // 4, lax.rem(patch, 4)


def neighbour(offset):
    z, x = place_on_torus()
    return lax.rem(z + offset[0] + 4, 4) * 4 + lax.rem(x + offset[1] + 4, 4)


def tap_rows(taps):
    half = taps.shape[-1] // 2

    def ring(v):
        gap = jnp.zeros(v.shape[:-1] + (128 - v.shape[-1],), v.dtype)
        return jnp.concatenate([v[..., half:], gap, v[..., :half]], -1)

    both = jnp.stack([ring(taps), ring(taps[..., ::-1])], 2)
    both = both.reshape(taps.shape[0], 4, 128).astype(F32)
    return jnp.pad(both, ((0, 0), (0, 4), (0, 0)))


def stamp_order(stamp_patch, stamp_band):
    z, x = place_on_torus()
    dz = lax.rem(stamp_patch // 4 - z + 4, 4)
    dx = lax.rem(lax.rem(stamp_patch, 4) - x + 4, 4)
    offset = dz * 4 + dx
    unit = jnp.zeros_like(offset)
    for number, (a, b) in enumerate(UNITS):
        unit = jnp.where(offset == (a % 4) * 4 + b % 4, number, unit)
    tile = unit * BANDS + stamp_band
    number = jnp.arange(STAMPS, dtype=jnp.int32)
    rank = tile * STAMPS + number
    before = rank[None, :] < rank[:, None]
    spot = jnp.sum(before.astype(jnp.int32), 1)
    mate = jnp.any(before & (tile[None, :] == tile[:, None]), 1).astype(jnp.int32)
    here = spot[None, :] == number[:, None]
    packed = (tile * STAMPS + number) * 2 + mate
    packed = jnp.sum(jnp.where(here, packed[None, :], 0), 1)
    tiles, ids, same = packed // (2 * STAMPS), lax.rem(packed // 2, STAMPS), lax.rem(packed, 2).astype(F32)
    every = jnp.arange(TILES, dtype=jnp.int32)
    upto = jnp.sum((tile[None, :] <= every[:, None]).astype(jnp.int32), 1)
    has = jnp.any(tile[None, :] == every[:, None], 1).astype(F32)
    return ids, tiles, same, jnp.maximum(upto - 1, 0), has


def build(row, dst):
    ring = pltpu.roll(jnp.broadcast_to(row, (128, 128)), 0, 1, stride=1, stride_axis=0)
    d = lax.broadcasted_iota(jnp.int32, (128, 128), 1) - lax.broadcasted_iota(
        jnp.int32, (128, 128), 0
    )
    zero = jnp.zeros_like(ring)
    diag = jnp.where(jnp.abs(d) < 64, ring, zero).astype(BF16)
    dst[0:128, 0:128] = diag
    dst[128:256, 128:256] = diag
    dst[112:128, 128:256] = jnp.where(d < -64, ring, zero)[112:].astype(BF16)
    dst[128:144, 0:128] = jnp.where(d > 64, ring, zero)[:16].astype(BF16)


def dot(a, b):
    return jnp.dot(a, b, preferred_element_type=F32)


def send(link, src, dst, send_sem, recv_sem):
    return pltpu.make_async_remote_copy(
        src_ref=src,
        dst_ref=dst,
        send_sem=send_sem,
        recv_sem=recv_sem,
        device_id={"patch": neighbour(LINKS[link])},
        device_id_type=MESH,
    )


def span(offset, half):
    first = UNIT[offset] * BANDS + half * HALF
    return slice(first, first + HALF)


def whole(offset):
    return slice(UNIT[offset] * BANDS, UNIT[offset] * BANDS + BANDS)


def flip(offset):
    return tuple(d if d == 2 else -d for d in offset)


def gather_copies(got, ssem, rsem):
    table = []
    for k, link in enumerate(LINKS):
        dz, dx = link
        along_x, sign = dz == 0, dz + dx
        back = flip(link)
        moves = [((0, 0), back, 0), ((0, 0), back, 1)]
        moves.append((back, (0, 2) if along_x else (2, 0), 0 if sign > 0 else 1))
        diag = []
        for s in (-sign, sign):
            diag.append(((s, 0), (s, -dx), 1) if along_x else ((0, s), (-dz, s), 0))
        far = ((2, 0), (2, -dx)) if along_x else ((0, 2), (-dz, 2))
        moves += [diag[0], (*far, 0), (*far, 1), diag[1]]
        row = [
            send(k, got.at[span(a, h)], got.at[span(b, h)], ssem.at[k, n], rsem.at[k, n])
            for n, (a, b, h) in enumerate(moves)
        ]
        rows = slice(k * 64, k * 64 + 64)
        row.append(
            send(k, got.at[whole(far[1]), rows], got.at[whole((2, 2)), rows], ssem.at[k, 7], rsem.at[k, 7])
        )
        table.append(row)
    return table


def main_kernel(ids, tls, same, last, has, gain, weight, rows, sky, pix, out, sq,
                got, tiles, pixv, seg, carry, mats, blur, resi, back, skyb,
                lsem, ssem, rsem, ssem2, rsem2, free):
    barrier = pltpu.get_barrier_semaphore()
    for link in LINKS:
        pl.semaphore_signal(
            barrier, inc=1, device_id={"patch": neighbour(link)}, device_id_type=MESH
        )
    sky_load = pltpu.make_async_copy(sky, skyb, lsem.at[0])
    sky_load.start()
    pix_load = pltpu.make_async_copy(pix, pixv, lsem.at[1])
    pix_load.start()
    sky_load.wait()

    @pl.loop(0, BANDS)
    def _(b):
        half = skyb[b].astype(BF16)
        got[b] = half
        tiles[b] = half

    pl.semaphore_wait(barrier, 4)
    moves = gather_copies(got, ssem, rsem)
    for k, link in enumerate(LINKS):
        for n in (0, 1) if sum(link) > 0 else (1, 0):
            moves[k][n].start()
    carry[...] = jnp.zeros_like(carry)
    mats[...] = jnp.zeros_like(mats)

    def keep(*offsets):
        for offset in offsets:

            @pl.loop(UNIT[offset] * BANDS, UNIT[offset] * BANDS + BANDS)
            def _(t):
                tiles[t] = got[t]

    def body(step, nothing):
        at = [step * PER + u for u in range(PER)]
        idx = [ids[a] for a in at]
        for u in range(PER):
            for m in range(4):
                build(rows[idx[u], m : m + 1, :], mats.at[u, m])
        g = [gain[i] for i in idx]
        w = [weight[i] for i in idx]
        for u in range(PER):
            blur[u] = dot(tiles[tls[at[u]]], mats[u, 3]).astype(BF16)
        for u in range(PER):
            predicted = g[u] * dot(mats[u, 0], blur[u])
            resi[u] = (w[u] * (predicted - pixv[idx[u]].astype(F32))).astype(BF16)
        for u in range(PER):
            back[u] = dot(mats[u, 1], resi[u]).astype(BF16)
        for u in range(PER):
            total = carry[...] * same[at[u]] + g[u] * dot(back[u], mats[u, 2])
            carry[...] = total
            seg[at[u]] = total.astype(BF16)
        return nothing

    def stamps(lo, hi):
        lax.fori_loop(lo // PER, hi // PER, body, 0)

    for k, link in enumerate(LINKS):
        moves[k][0 if sum(link) > 0 else 1].wait_recv()
    for k in range(4):
        moves[k][2].start()
    for k, link in enumerate(LINKS):
        moves[k][1 if sum(link) > 0 else 0].wait_recv()
    for k in range(4):
        moves[k][3].start()
    keep(*UNITS[1:5])
    pix_load.wait()
    for k in range(4):
        moves[k][2].wait_recv()
    for k in range(4):
        for n in (4, 5, 6):
            moves[k][n].start()
    keep(*UNITS[5:7])
    stamps(0, 20)
    for k in range(4):
        moves[k][3].wait_recv()
    keep(*UNITS[7:9])
    stamps(20, 44)
    for k in range(4):
        moves[k][4].wait_recv()
        moves[k][5].wait_recv()
        moves[k][7].start()
    keep(*UNITS[9:13])
    stamps(44, 92)
    for k in range(4):
        moves[k][6].wait_recv()
        moves[k][7].wait_recv()
    keep(*UNITS[13:16])
    for k in range(4):
        for n in range(8):
            moves[k][n].wait_send()
    for link in LINKS:
        pl.semaphore_signal(free, inc=1, device_id={"patch": neighbour(link)}, device_id_type=MESH)
    stamps(92, 128)

    def collect(lo, hi):
        @pl.loop(lo * BANDS, hi * BANDS)
        def _(t):
            tiles[t] = (seg[last[t]].astype(F32) * has[t]).astype(BF16)

    copies, info = [], []
    for k, link in enumerate(LINKS):
        dz, dx = link
        late = 0 if dz + dx > 0 else 1
        early = 1 - late
        along_x = dz == 0
        far = (2, dx) if along_x else (dz, 2)
        straight = (0, 2) if along_x else (2, 0)
        sides = [(s, dx) if along_x else (dz, s) for s in (1, -1)]
        diag_half = 1 if along_x else 0
        rows_k = slice(k * 64, k * 64 + 64)
        diag, three, two, one = 6 + 6 * k, 30 + 6 * k, 54 + 3 * k, 66 + 6 * k
        row = [send(k, tiles.at[whole((2, 2)), rows_k], got.at[0:6, rows_k], ssem2.at[k, 0], rsem2.at[k, 0])]
        for n, (offset, h, dst) in enumerate(
            [
                (sides[0], diag_half, diag),
                (far, 0, three),
                (far, 1, three + 3),
                (sides[1], diag_half, diag + 3),
                (straight, late, two),
                (link, early, one + early * 3),
                (link, late, one + late * 3),
            ],
            1,
        ):
            row.append(send(k, tiles.at[span(offset, h)], got.at[dst : dst + 3], ssem2.at[k, n], rsem2.at[k, n]))
        copies.append(row)
        info.append((far, straight, sides, diag_half, early, late, diag, three, two, one))

    def add_into(slots, src):
        @pl.loop(0, HALF)
        def _(t):
            d = slots.start + t
            tiles[d] = (tiles[d].astype(F32) + got[src + t].astype(F32)).astype(BF16)

    collect(15, 16)
    pl.semaphore_wait(free, 4)
    for k in range(4):
        copies[k][0].start()
    collect(7, 15)
    for k in range(4):
        copies[k][1].start()
    for k in range(4):
        copies[k][0].wait_recv()
        first = UNIT[info[k][0]] * BANDS

        @pl.loop(0, BANDS)
        def _(b):
            r = slice(k * 64, k * 64 + 64)
            tiles[first + b, r] = (tiles[first + b, r].astype(F32) + got[b, r].astype(F32)).astype(BF16)

        for n in (2, 3, 4):
            copies[k][n].start()
    collect(0, 7)
    for h in range(2):
        for k in range(4):
            copies[k][2 + h].wait_recv()
            target = (2, 0) if LINKS[k][0] == 0 else (0, 2)
            add_into(span(target, h), info[k][7] + h * HALF)
        for k in range(4):
            if info[k][5] == h:
                copies[k][5].start()
    for k in range(4):
        sides, diag_half = info[k][2:4]
        for s in range(2):
            copies[k][1 if s == 0 else 4].wait_recv()
            dz, dx = sides[s]
            target = (dz, 0) if LINKS[k][0] == 0 else (0, dx)
            add_into(span(target, diag_half), info[k][6] + s * HALF)
    for k in range(4):
        copies[k][6].start()
    for k in range(4):
        copies[k][5].wait_recv()
        add_into(span(LINKS[k], info[k][5]), info[k][8])
        copies[k][7].start()
    for k in range(4):
        copies[k][6].wait_recv()
        copies[k][7].wait_recv()

    def finish(b, total):
        gradient = tiles[b].astype(F32)
        for k in range(4):
            gradient = gradient + got[info[k][9] + b].astype(F32)
        step_field = STEP_RATE * gradient
        skyb[b] = skyb[b] - step_field
        squares = (step_field * step_field).reshape(TS // 8, 8, TS).sum(0)
        return total + squares[:, :128] + squares[:, 128:]

    sq[...] = lax.fori_loop(0, BANDS, finish, jnp.zeros((8, 128), F32))
    c = pltpu.make_async_copy(skyb, out, lsem.at[0])
    c.start()
    for k in range(4):
        for c2 in copies[k]:
            c2.wait_send()
    c.wait()


def step(order, gain, weight, rows, sky, pix):
    smem = pl.BlockSpec(memory_space=pltpu.SMEM)
    anys = pl.BlockSpec(memory_space=pl.ANY)
    vmem = pl.BlockSpec(memory_space=pltpu.VMEM)
    return pl.pallas_call(
        main_kernel,
        out_shape=(
            jax.ShapeDtypeStruct((BANDS, TS, TS), F32),
            jax.ShapeDtypeStruct((8, 128), F32),
        ),
        in_specs=[smem] * 7 + [vmem, anys, anys],
        out_specs=(anys, vmem),
        scratch_shapes=[
            pltpu.VMEM((TILES, TS, TS), BF16),
            pltpu.VMEM((TILES, TS, TS), BF16),
            pltpu.VMEM((STAMPS, TS, TS), BF16),
            pltpu.VMEM((STAMPS, TS, TS), BF16),
            pltpu.VMEM((TS, TS), F32),
            pltpu.VMEM((PER, 4, TS, TS), BF16),
            pltpu.VMEM((PER, TS, TS), BF16),
            pltpu.VMEM((PER, TS, TS), BF16),
            pltpu.VMEM((PER, TS, TS), BF16),
            pltpu.VMEM((BANDS, TS, TS), F32),
            pltpu.SemaphoreType.DMA((2,)),
            pltpu.SemaphoreType.DMA((4, 8)),
            pltpu.SemaphoreType.DMA((4, 8)),
            pltpu.SemaphoreType.DMA((4, 8)),
            pltpu.SemaphoreType.DMA((4, 8)),
            pltpu.SemaphoreType.REGULAR,
        ],
        compiler_params=pltpu.CompilerParams(
            collective_id=1, has_side_effects=True, vmem_limit_bytes=63 * 2**20 + 2**19
        ),
        name="step",
    )(*order, gain, weight, rows, sky, pix)


def total_kernel(sq, out, held, ssem, rsem):
    patch, exp = lax.axis_index("patch"), lax.axis_index("exp")
    z, x = patch // 4, lax.rem(patch, 4)
    y, core = exp // 2, lax.rem(exp, 2)
    rounds = [
        (core, [("exp", exp + 1 - 2 * core)]),
        (x, [("patch", z * 4 + lax.rem(x + d, 4)) for d in (1, 2, 3)]),
        (z, [("patch", lax.rem(z + d, 4) * 4 + x) for d in (1, 2, 3)]),
        (y, [("exp", lax.rem(y + d, 4) * 2 + core) for d in (1, 2, 3)]),
    ]
    barrier = pltpu.get_barrier_semaphore()
    for _, peers in rounds:
        for peer in peers:
            pl.semaphore_signal(barrier, inc=1, device_id=dict([peer]), device_id_type=MESH)
    total = jnp.sum(sq[...], 0, keepdims=True)
    total = jnp.broadcast_to(total, (8, 128))
    pl.semaphore_wait(barrier, 10)
    for n, (place, peers) in enumerate(rounds):
        held[n, place] = total
        copies = [
            pltpu.make_async_remote_copy(
                src_ref=held.at[n, place], dst_ref=held.at[n, place],
                send_sem=ssem.at[n, k], recv_sem=rsem.at[n, k],
                device_id=dict([peer]), device_id_type=MESH,
            )
            for k, peer in enumerate(peers)
        ]
        for c in copies:
            c.start()
        for c in copies:
            c.wait()
        total = held[n, 0]
        for k in range(1, len(peers) + 1):
            total = total + held[n, k]
    total = jnp.sum(total[0:1], 1, keepdims=True)
    count = 16 * 8 * BANDS * TS * TS
    out[...] = jnp.broadcast_to(jnp.sqrt(total / count + 1e-06), (8, 128))


def total_of(sq):
    vmem = pl.BlockSpec(memory_space=pltpu.VMEM)
    return pl.pallas_call(
        total_kernel,
        out_shape=jax.ShapeDtypeStruct((8, 128), F32),
        in_specs=[vmem],
        out_specs=vmem,
        scratch_shapes=[
            pltpu.VMEM((4, 4, 8, 128), F32),
            pltpu.SemaphoreType.DMA((4, 3)),
            pltpu.SemaphoreType.DMA((4, 3)),
        ],
        compiler_params=pltpu.CompilerParams(collective_id=2, has_side_effects=True),
        name="total",
    )(sq)


def per_device(
    sky_model, stamp_pixels, stamp_patch, stamp_band, psf_taps, stamp_gain, stamp_weight
):
    sky = sky_model.reshape(BANDS, TS, TS)
    order = stamp_order(stamp_patch[:, 0], stamp_band)
    rows = tap_rows(psf_taps)
    gain, weight = stamp_gain.astype(F32), stamp_weight.astype(F32)
    new_model, squares = step(order, gain, weight, rows, sky, stamp_pixels)
    return (new_model.reshape(sky_model.shape), total_of(squares)[0, 0])


def solution(mesh):
    return jax.shard_map(
        per_device,
        mesh=mesh,
        in_specs=(
            P("patch", "exp", None, None, None),
            P(("patch", "exp"), None, None),
            P(("patch", "exp"), None),
            P(("patch", "exp")),
            P(("patch", "exp"), None, None),
            P(("patch", "exp")),
            P(("patch", "exp")),
        ),
        out_specs=(P("patch", "exp", None, None, None), P()),
        check_vma=False,
    )
```

time: 559 us -> 180 us (0.32)
  waiting for transfers between devices: 185 us -> 0 us
  Pallas kernels: 0 us -> 165 us
  matrix products: 119 us -> 0 us
  other arithmetic: 95.3 us -> 6.46 us
  local copies, waits for them, and re-layouts: 77 us -> 6.64 us
  blocking collectives: 64.5 us -> 0 us
  between operations: 15.9 us -> 0.74 us
    pallas_call x0 -> x2, Pallas kernels: none -> 165 us  [the longest x1 149 us: step(): pl.pallas_call(main_kernel, out_shape=(jax.ShapeDtypeStruct((BANDS, TS, T...]
    dot_general x20 -> x0, matrix products: 119 us -> none  [the longest x4 42.6 us: stamp_adjoint(): jnp.einsum('sba,sbc->sac', row_kernel, residual, preferred_element_type=j...]
    unnamed x3 -> x0, waiting for transfers between devices: 94 us -> none
    all_gather x1 -> x0, waiting for transfers between devices: 91.4 us -> none  [per_device(): gathered = lax.all_gather(model_half, 'patch', axis=0, tiled=True)]
    scatter-add x4 -> x0, other arithmetic: 75.6 us -> none  [source_block(): return (running.at[keys_block].add(adjoint), None)]
    psum x1 -> x0, blocking collectives: 64.5 us -> none  [per_device(): square_sum = lax.psum(jnp.sum(step_field * step_field), ('patch', 'exp'))]
    convert_element_type x4 -> x0, local copies, waits for them, and re-layouts: 30.1 us -> none  [banded_matrices(): return jnp.einsum('sk,kij->sij', tap_values, tap_table, preferred_element...]
    gather x4 -> x0, local copies, waits for them, and re-layouts: 29.4 us -> none  [source_block(): tile_sel = jnp.take(flat_tiles, keys_block, axis=0)]
  transfers between devices with their start and end apart: 2 -> 0, of which waited for: 2 -> 0; matrix products, arithmetic and copies ran while one was open for 1% -> 0% of each run, Pallas kernels for 0% -> 0%
where the time goes in v2:
time: 180 us; the launch traced here: 179 us
  Pallas kernels  165 us (92%)
  local copies, waits for them, and re-layouts  6.64 us (4%)
  other arithmetic  6.46 us (4%)
    pallas_call x1, Pallas kernels, step(): pl.pallas_call(main_kernel, out_shape=(jax.ShapeDtypeStruct((BANDS, TS, T...  149 us
    pallas_call x1, Pallas kernels, total_of(): pl.pallas_call(total_kernel, out_shape=jax.ShapeDtypeStruct((8, 128), F32...  15.5 us

profile of v2, /device:TPU:1, one launch (start us, length us, event | category | flops | bytes accessed | tf_op | source)
XLA Modules:
  0.0 178.5 jit_solution(8504021849821269109)
XLA Ops:
  0.6 0.7 iota_add_fusion
  1.3 0.2 fusion.1
  1.5 0.2 fusion
  1.7 0.1 select_reduce_fusion
  1.8 0.1 fusion.2
  2.0 0.1 convert_reduce_fusion
  2.1 0.6 add_maximum_fusion.last
  2.7 0.5 convert_element_type.31.has
  3.1 1.2 convert_element_type.32.gain
  4.4 1.2 convert_element_type.33.weight
  5.6 0.1 pad.14.clone
  5.7 0.6 fusion.10
  6.3 0.7 fusion.13
  7.0 0.8 fusion.12
  7.8 0.1 copy.19
  7.9 0.1 copy.20
  8.0 0.1 copy.21
  8.2 0.2 slice.24
  8.4 0.1 copy.22
  8.5 0.2 slice.26
  8.8 0.1 maximum_bitcast_fusion
  8.9 0.1 copy.23
  9.1 0.8 pad_convert_fusion.rows
  9.9 149.2 %step.1 = (f32[6,256,256]{2,1,0:T(8,128)}, f32[8,128]{1,0:T(8,128)}) custom-call(s32[128]{0:T(128)} %get-tuple-element.16.ids, s32[128]{0:T(128)} %get-tuple-element.15.tls, f32[128]{0:T(128)} %get-tuple-element.14.same, s32[96]{0:T(128)} %add_maximum_fusion.last, f32[96]{0:T(128)} %convert_element_type.31.has, f32[128]{0:T(128)} %convert_element_type.32.gain, ...), custom_call_target="tpu_custom_call" | custom-call | tf_op jit(solution)/shard_map/step/pallas_call | solution.py:344
  159.1 15.5 %total.1 = f32[8,128]{1,0:T(8,128)} custom-call(f32[8,128]{1,0:T(8,128)} %get-tuple-element.5.sq), custom_call_target="tpu_custom_call" | custom-call | tf_op jit(solution)/shard_map/total/pallas_call | solution.py:418
  174.6 1.2 slice.27
  175.8 2.7 %copy.25 = f32[1,1,6,256,256]{4,3,2,1,0:T(8,128)} copy(f32[1,1,6,256,256]{4,3,2,1,0:T(8,128)} %bitcast.23) | data formatting | bytes 3145728
  (3 shorter events, 0.0 us)

commit v3 on v2

v3 whole, which is shorter than its diff:
```python
import functools

import jax
import jax.numpy as jnp
from jax import lax
from jax.experimental import pallas as pl
from jax.experimental.pallas import tpu as pltpu
from jax.sharding import PartitionSpec as P

TS = 256
BANDS = 6
HALF = 3
STAMPS = 128
STEP_RATE = 0.2
F32, BF16 = jnp.float32, jnp.bfloat16
MESH = pl.DeviceIdType.MESH

UNITS = [
    (0, 0), (0, 1), (0, -1), (1, 0), (-1, 0),
    (1, -1), (-1, 1), (0, 2), (2, 0), (1, 1), (-1, -1),
    (2, 1), (1, 2), (2, -1), (-1, 2), (2, 2),
]
UNIT = {offset: number for number, offset in enumerate(UNITS)}
TILES = len(UNITS) * BANDS
LINKS = [(0, 1), (0, -1), (1, 0), (-1, 0)]
PER = 4


def place_on_torus():
    patch = lax.axis_index("patch")
    return patch // 4, lax.rem(patch, 4)


def neighbour(offset):
    z, x = place_on_torus()
    return lax.rem(z + offset[0] + 4, 4) * 4 + lax.rem(x + offset[1] + 4, 4)


def index_grids():
    return (
        lax.broadcasted_iota(jnp.int32, (128, 128), 0),
        lax.broadcasted_iota(jnp.int32, (128, 128), 1),
    )


def tap_rows(taps, rows):
    source, lane = index_grids()
    tap = jnp.where(lane <= 10, lane + 10, lane - 118)
    used = (lane <= 10) | (lane >= 118)
    for m in range(4):
        wanted = (20 - tap if m % 2 else tap) + 21 * (m // 2)
        pick = jnp.where(used & (source == wanted), 1.0, 0.0).astype(BF16)
        rows[m] = dot(taps[...], pick)


def stamp_order(patch, band, gain, weight, ints, floats):
    z, x = place_on_torus()
    down, lane = index_grids()

    def across(line):
        return jnp.broadcast_to(line, (128, 128))

    def total(grid):
        return jnp.sum(grid, 0, keepdims=True)

    where = across(patch[...])
    dz = lax.rem(where // 4 - z + 4, 4)
    dx = lax.rem(lax.rem(where, 4) - x + 4, 4)
    offset = dz * 4 + dx
    unit = jnp.zeros_like(offset)
    for number, (a, b) in enumerate(UNITS):
        unit = jnp.where(offset == (a % 4) * 4 + b % 4, number, unit)
    tile_d = unit * BANDS + across(band[...]).T
    tile_l = tile_d.T
    rank_d, rank_l = tile_d * STAMPS + down, tile_l * STAMPS + lane
    before = rank_d < rank_l
    one, none = jnp.ones_like(down), jnp.zeros_like(down)
    spot = across(total(jnp.where(before, one, none))).T
    mates = across(total(jnp.where(before & (tile_d == tile_l), one, none))).T
    here = spot == lane
    ints[0:1, :] = total(jnp.where(here, down, none))
    ints[1:2, :] = total(jnp.where(here, tile_d, none))
    ints[2:3, :] = jnp.maximum(total(jnp.where(tile_d <= lane, one, none)) - 1, 0)
    zero = jnp.zeros((128, 128), F32)
    floats[0:1, :] = total(jnp.where(here & (mates > 0), zero + 1.0, zero))
    floats[1:2, :] = jnp.where(total(jnp.where(tile_d == lane, one, none)) > 0, 1.0, 0.0)
    floats[2:3, :] = total(jnp.where(here, across(gain[...].astype(F32)).T, zero))
    floats[3:4, :] = total(jnp.where(here, across(weight[...].astype(F32)).T, zero))


def build(row, dst):
    ring = pltpu.roll(jnp.broadcast_to(row, (128, 128)), 0, 1, stride=1, stride_axis=0)
    d = lax.broadcasted_iota(jnp.int32, (128, 128), 1) - lax.broadcasted_iota(
        jnp.int32, (128, 128), 0
    )
    zero = jnp.zeros_like(ring)
    diag = jnp.where(jnp.abs(d) < 64, ring, zero).astype(BF16)
    dst[0:128, 0:128] = diag
    dst[128:256, 128:256] = diag
    dst[112:128, 128:256] = jnp.where(d < -64, ring, zero)[112:].astype(BF16)
    dst[128:144, 0:128] = jnp.where(d > 64, ring, zero)[:16].astype(BF16)


def dot(a, b):
    return jnp.dot(a, b, preferred_element_type=F32)


def send(link, src, dst, send_sem, recv_sem):
    return pltpu.make_async_remote_copy(
        src_ref=src,
        dst_ref=dst,
        send_sem=send_sem,
        recv_sem=recv_sem,
        device_id={"patch": neighbour(LINKS[link])},
        device_id_type=MESH,
    )


def span(offset, half):
    first = UNIT[offset] * BANDS + half * HALF
    return slice(first, first + HALF)


def whole(offset):
    return slice(UNIT[offset] * BANDS, UNIT[offset] * BANDS + BANDS)


def seen_from(link, offset):
    dz, dx = ((a - b + 1) % 4 - 1 for a, b in zip(offset, link))
    return dz, dx


FAR = [
    [((1, -1), 1), ((2, 0), 0)],
    [((2, 0), 0), ((-1, 1), 1)],
    [((-1, 1), 1), ((0, 2), 0)],
    [((0, 2), 0), ((1, -1), 1)],
]


def gather_copies(got, ssem, rsem):
    table = []
    for k, link in enumerate(LINKS):
        dz, dx = link
        along_x, sign = dz == 0, dz + dx
        diag = [((s, 0), 1) if along_x else ((0, s), 0) for s in (sign, -sign)]
        straight = ((-dz, -dx), 0 if sign > 0 else 1)
        moves = [((0, 0), 0), ((0, 0), 1), diag[0], straight, diag[1], *FAR[k]]
        row = [
            send(k, got.at[span(a, h)], got.at[span(seen_from(link, a), h)], ssem.at[k, n], rsem.at[k, n])
            for n, (a, h) in enumerate(moves)
        ]
        rows = slice(k * 64, k * 64 + 64)
        via = (2, -dx) if along_x else (-dz, 2)
        row.append(
            send(k, got.at[whole(via), rows], got.at[whole((2, 2)), rows], ssem.at[k, 7], rsem.at[k, 7])
        )
        table.append(row)
    return table


def reduce_copies(tiles, got, ssem, rsem):
    copies, info = [], []
    for k, link in enumerate(LINKS):
        dz, dx = link
        late = 0 if dz + dx > 0 else 1
        early = 1 - late
        along_x = dz == 0
        far = (2, dx) if along_x else (dz, 2)
        straight = (0, 2) if along_x else (2, 0)
        sides = [(s, dx) if along_x else (dz, s) for s in (-dz - dx, dz + dx)]
        diag_half = 1 if along_x else 0
        rows_k = slice(k * 64, k * 64 + 64)
        diag, three, two, one = 6 + 6 * k, 30 + 6 * k, 54 + 3 * k, 66 + 6 * k
        row = [send(k, tiles.at[whole((2, 2)), rows_k], got.at[0:6, rows_k], ssem.at[k, 0], rsem.at[k, 0])]
        for n, (offset, h, dst) in enumerate(
            [
                (sides[0], diag_half, diag),
                (far, 0, three),
                (far, 1, three + 3),
                (sides[1], diag_half, diag + 3),
                (straight, late, two),
                (link, early, one + early * 3),
                (link, late, one + late * 3),
            ],
            1,
        ):
            row.append(send(k, tiles.at[span(offset, h)], got.at[dst : dst + 3], ssem.at[k, n], rsem.at[k, n]))
        copies.append(row)
        info.append((far, straight, sides, diag_half, early, late, diag, three, two, one))

    return copies, info


def main_kernel(patch_of, band_of, gain_of, weight_of, taps, sky, pix, out, rms,
                got, tiles, pixv, seg, carry, mats, blur, resi, back, skyb, rows, intv, floatv, ints, floats, held, held2,
                lsem, ssem, rsem, ssem2, rsem2, tsem, tsem2, tsem3, tsem4, early, free):
    patch, exp = lax.axis_index("patch"), lax.axis_index("exp")
    peers = [{"patch": lax.rem(patch + k, 16)} for k in range(1, 16)]
    peers2 = [{"exp": lax.rem(exp + k, 8)} for k in range(1, 8)]
    barrier = pltpu.get_barrier_semaphore()
    for peer in peers + peers2:
        pl.semaphore_signal(barrier, inc=1, device_id=peer, device_id_type=MESH)
    sky_load = pltpu.make_async_copy(sky, skyb, lsem.at[0])
    sky_load.start()
    pix_load = pltpu.make_async_copy(pix, pixv, lsem.at[1])
    pix_load.start()
    sky_load.wait()

    @pl.loop(0, BANDS)
    def _(b):
        half = skyb[b].astype(BF16)
        got[b] = half
        tiles[b] = half

    pl.semaphore_wait(barrier, len(peers) + len(peers2))
    moves = gather_copies(got, ssem, rsem)
    for k, link in enumerate(LINKS):
        for n in (0, 1) if link[0] == 0 else (1, 0):
            moves[k][n].start()
    stamp_order(patch_of, band_of, gain_of, weight_of, intv, floatv)
    tables = [
        pltpu.make_async_copy(intv, ints, lsem.at[2]),
        pltpu.make_async_copy(floatv, floats, lsem.at[3]),
    ]
    for c in tables:
        c.start()
    tap_rows(taps, rows)
    carry[...] = jnp.zeros_like(carry)
    mats[...] = jnp.zeros_like(mats)

    def keep(*offsets):
        for offset in offsets:

            @pl.loop(UNIT[offset] * BANDS, UNIT[offset] * BANDS + BANDS)
            def _(t):
                tiles[t] = got[t]

    def body(step, nothing):
        at = [step * PER + u for u in range(PER)]
        idx = [ints[0, a] for a in at]
        for u in range(PER):
            for m in range(4):
                build(rows[m, pl.ds(idx[u], 1), :], mats.at[u, m])
        g = [floats[2, a] for a in at]
        w = [floats[3, a] for a in at]
        for u in range(PER):
            blur[u] = dot(tiles[ints[1, at[u]]], mats[u, 3]).astype(BF16)
        for u in range(PER):
            predicted = g[u] * dot(mats[u, 0], blur[u])
            resi[u] = (w[u] * (predicted - pixv[idx[u]].astype(F32))).astype(BF16)
        for u in range(PER):
            back[u] = dot(mats[u, 1], resi[u]).astype(BF16)
        for u in range(PER):
            total = carry[...] * floats[0, at[u]] + g[u] * dot(back[u], mats[u, 2])
            carry[...] = total
            seg[at[u]] = total.astype(BF16)
        return nothing

    def stamps(lo, hi):
        lax.fori_loop(lo // PER, hi // PER, body, 0)

    def collect(lo, hi):
        @pl.loop(lo * BANDS, hi * BANDS)
        def _(t):
            tiles[t] = (seg[ints[2, t]].astype(F32) * floats[1, t]).astype(BF16)

    def tell(semaphore):
        for link in LINKS:
            pl.semaphore_signal(
                semaphore, inc=1, device_id={"patch": neighbour(link)}, device_id_type=MESH
            )

    copies, info = reduce_copies(tiles, got, ssem2, rsem2)

    def arrive(*numbers):
        for k in range(4):
            for n in numbers:
                moves[k][n].wait_recv()

    def forward(*numbers):
        for k in range(4):
            for n in numbers:
                moves[k][n].start()

    def gone(*numbers):
        for k in range(4):
            for n in numbers:
                moves[k][n].wait_send()

    for k, link in enumerate(LINKS):
        moves[k][0 if link[0] == 0 else 1].wait_recv()
    forward(2)
    for k, link in enumerate(LINKS):
        moves[k][1 if link[0] == 0 else 0].wait_recv()
    forward(3, 4)
    keep(*UNITS[1:5])
    for c in tables:
        c.wait()
    pix_load.wait()
    arrive(2)
    keep(*UNITS[5:7])
    stamps(0, 20)
    arrive(3)
    forward(5, 6)
    keep(*UNITS[7:9])
    stamps(20, 44)
    arrive(4)
    keep(*UNITS[9:11])
    stamps(44, 68)
    arrive(5)
    for k in (1, 3):
        moves[k][7].start()
    keep(*UNITS[11:13])
    gone(2, 3, 4)
    tell(early)
    stamps(68, 92)
    arrive(6)
    for k in (0, 2):
        moves[k][7].start()
    keep(*UNITS[13:15])
    collect(5, 7)
    pl.semaphore_wait(early, 4)
    for k in range(4):
        copies[k][1].start()
    stamps(92, 116)
    arrive(7)
    keep(*UNITS[15:16])
    gone(0, 1, 5, 6, 7)
    tell(free)
    stamps(116, 128)

    def add_into(slots, src):
        @pl.loop(0, HALF)
        def _(t):
            d = slots.start + t
            tiles[d] = (tiles[d].astype(F32) + got[src + t].astype(F32)).astype(BF16)

    collect(15, 16)
    pl.semaphore_wait(free, 4)
    for k in range(4):
        copies[k][0].start()
    collect(9, 15)
    for k in range(4):
        copies[k][0].wait_recv()
        first = UNIT[info[k][0]] * BANDS

        @pl.loop(0, BANDS)
        def _(b):
            r = slice(k * 64, k * 64 + 64)
            tiles[first + b, r] = (tiles[first + b, r].astype(F32) + got[b, r].astype(F32)).astype(BF16)

        for n in (2, 3, 4):
            copies[k][n].start()
    collect(0, 5)
    collect(7, 9)
    for h in range(2):
        for k in range(4):
            copies[k][2 + h].wait_recv()
            target = (2, 0) if LINKS[k][0] == 0 else (0, 2)
            add_into(span(target, h), info[k][7] + h * HALF)
        for k in range(4):
            if info[k][5] == h:
                copies[k][5].start()
    for k in range(4):
        sides, diag_half = info[k][2:4]
        for s in range(2):
            copies[k][1 if s == 0 else 4].wait_recv()
            dz, dx = sides[s]
            target = (dz, 0) if LINKS[k][0] == 0 else (0, dx)
            add_into(span(target, diag_half), info[k][6] + s * HALF)
    for k in range(4):
        copies[k][6].start()
    for k in range(4):
        copies[k][5].wait_recv()
        add_into(span(LINKS[k], info[k][5]), info[k][8])
        copies[k][7].start()
    for k in range(4):
        copies[k][6].wait_recv()
        copies[k][7].wait_recv()

    def finish(b, total):
        gradient = tiles[b].astype(F32)
        for k in range(4):
            gradient = gradient + got[info[k][9] + b].astype(F32)
        step_field = STEP_RATE * gradient
        skyb[b] = skyb[b] - step_field
        squares = (step_field * step_field).reshape(TS // 8, 8, TS).sum(0)
        return total + squares[:, :128] + squares[:, 128:]

    squares = lax.fori_loop(0, BANDS, finish, jnp.zeros((8, 128), F32))
    c = pltpu.make_async_copy(skyb, out, lsem.at[0])
    c.start()

    def exchange(slots, place, value, devices, send_sems, recv_sems):
        slots[place] = value
        shares = [
            pltpu.make_async_remote_copy(
                src_ref=slots.at[place],
                dst_ref=slots.at[place],
                send_sem=send_sems.at[k],
                recv_sem=recv_sems.at[k],
                device_id=device,
                device_id_type=MESH,
            )
            for k, device in enumerate(devices)
        ]
        for share in shares:
            share.start()
        for share in shares:
            share.wait()
        return jnp.sum(slots[...], 0)

    squares = exchange(held, patch, squares, peers, tsem, tsem2)
    squares = exchange(held2, exp, squares, peers2, tsem3, tsem4)
    mean = jnp.sum(jnp.sum(squares, 0, keepdims=True), 1, keepdims=True) / (128 * BANDS * TS * TS)
    rms[...] = jnp.broadcast_to(jnp.sqrt(mean + 1e-06), rms.shape)
    for k in range(4):
        for c2 in copies[k]:
            c2.wait_send()
    c.wait()


def step(patch, band, gain, weight, taps, sky, pix):
    anys = pl.BlockSpec(memory_space=pl.ANY)
    vmem = pl.BlockSpec(memory_space=pltpu.VMEM)
    return pl.pallas_call(
        main_kernel,
        out_shape=(
            jax.ShapeDtypeStruct((BANDS, TS, TS), F32),
            jax.ShapeDtypeStruct((1, 128), F32),
        ),
        in_specs=[vmem] * 5 + [anys, anys],
        out_specs=(anys, vmem),
        scratch_shapes=[
            pltpu.VMEM((TILES, TS, TS), BF16),
            pltpu.VMEM((TILES, TS, TS), BF16),
            pltpu.VMEM((STAMPS, TS, TS), BF16),
            pltpu.VMEM((STAMPS, TS, TS), BF16),
            pltpu.VMEM((TS, TS), F32),
            pltpu.VMEM((PER, 4, TS, TS), BF16),
            pltpu.VMEM((PER, TS, TS), BF16),
            pltpu.VMEM((PER, TS, TS), BF16),
            pltpu.VMEM((PER, TS, TS), BF16),
            pltpu.VMEM((BANDS, TS, TS), F32),
            pltpu.VMEM((4, 128, 128), F32),
            pltpu.VMEM((8, 128), jnp.int32),
            pltpu.VMEM((8, 128), F32),
            pltpu.SMEM((8, 128), jnp.int32),
            pltpu.SMEM((8, 128), F32),
            pltpu.VMEM((16, 8, 128), F32),
            pltpu.VMEM((8, 8, 128), F32),
            pltpu.SemaphoreType.DMA((4,)),
            pltpu.SemaphoreType.DMA((4, 8)),
            pltpu.SemaphoreType.DMA((4, 8)),
            pltpu.SemaphoreType.DMA((4, 8)),
            pltpu.SemaphoreType.DMA((4, 8)),
            pltpu.SemaphoreType.DMA((15,)),
            pltpu.SemaphoreType.DMA((15,)),
            pltpu.SemaphoreType.DMA((7,)),
            pltpu.SemaphoreType.DMA((7,)),
            pltpu.SemaphoreType.REGULAR,
            pltpu.SemaphoreType.REGULAR,
        ],
        compiler_params=pltpu.CompilerParams(
            collective_id=1, has_side_effects=True, vmem_limit_bytes=63 * 2**20 + 2**19
        ),
        name="step",
    )(patch, band, gain, weight, taps, sky, pix)


def per_device(
    sky_model, stamp_pixels, stamp_patch, stamp_band, psf_taps, stamp_gain, stamp_weight
):
    sky = sky_model.reshape(BANDS, TS, TS)
    taps = jnp.pad(psf_taps.reshape(STAMPS, -1), ((0, 0), (0, 128 - 2 * psf_taps.shape[-1])))
    band, gain, weight = (v.reshape(1, STAMPS) for v in (stamp_band, stamp_gain, stamp_weight))
    new_model, rms = step(stamp_patch, band, gain, weight, taps, sky, stamp_pixels)
    return (new_model.reshape(sky_model.shape), rms[0, 0])


def solution(mesh):
    return jax.shard_map(
        per_device,
        mesh=mesh,
        in_specs=(
            P("patch", "exp", None, None, None),
            P(("patch", "exp"), None, None),
            P(("patch", "exp"), None),
            P(("patch", "exp")),
            P(("patch", "exp"), None, None),
            P(("patch", "exp")),
            P(("patch", "exp")),
        ),
        out_specs=(P("patch", "exp", None, None, None), P()),
        check_vma=False,
    )
```

time: 180 us -> 158 us (0.88)
  Pallas kernels: 165 us -> 151 us
  other arithmetic: 6.46 us -> 0 us
    pallas_call x1 -> x0, Pallas kernels: 15.5 us -> none  [total_of(): pl.pallas_call(total_kernel, out_shape=jax.ShapeDtypeStruct((8, 128), F32...]
    slice x9 -> x0, local copies, waits for them, and re-layouts: 3.69 us -> none  [the longest x8 2.49 us: ring(): return jnp.concatenate([v[..., half:], gap, v[..., :half]], -1)]
    convert_element_type x4 -> x0, other arithmetic: 3.5 us -> none  [the longest x2 2.43 us: per_device(): gain, weight = (stamp_gain.astype(F32), stamp_weight.astype(F32))]
    unnamed x1 -> x5, local copies, waits for them, and re-layouts: 2.73 us -> 4.84 us
where the time goes in v3:
time: 158 us
  Pallas kernels  151 us (96%)
  local copies, waits for them, and re-layouts  5.59 us (4%)
  between operations  1.81 us (1%)
    pallas_call x1, Pallas kernels, step(): pl.pallas_call(main_kernel, out_shape=(jax.ShapeDtypeStruct((BANDS, TS, T...  151 us
    unnamed x5, local copies, waits for them, and re-layouts  4.84 us

profile of v3, /device:TPU:1, one launch (start us, length us, event | category | flops | bytes accessed | tf_op | source)
XLA Modules:
  0.0 158.2 jit_solution(5388820600769377373)
XLA Ops:
  0.6 0.7 copy.11
  1.3 0.1 copy.12
  1.5 0.6 pad.4.taps
  2.1 1.4 copy.13.patch_of
  3.5 150.8 %step.1 = (f32[6,256,256]{2,1,0:T(8,128)}, f32[1,128]{1,0:T(1,128)}) custom-call(s32[128,1]{1,0:T(8,128)} %copy.13.patch_of, s32[1,128]{1,0:T(1,128)} %bitcast.11, bf16[1,128]{1,0:T(2,128)(2,1)} %bitcast.12, bf16[1,128]{1,0:T(2,128)(2,1)} %bitcast.13, bf16[128,128]{1,0:T(8,128)(2,1)} %pad.4.taps, f32[6,256,256]{2,1,0:T(8,128)} %bitcast.10, ...), custom_call_target="tpu_custom_call" | custom-call | tf_op jit(solution)/shard_map/step/pallas_call | solution.py:427
  154.3 0.0 copy-start
  154.3 2.7 %copy.16 = f32[1,1,6,256,256]{4,3,2,1,0:T(8,128)} copy(f32[1,1,6,256,256]{4,3,2,1,0:T(8,128)} %bitcast.9) | data formatting | bytes 3145728
  157.0 0.0 copy-done
  (1 shorter events, 0.0 us)
Async XLA Ops:
  154.3 2.7 %copy-start = (f32[1,128]{1,0:T(1,128)S(1)}, f32[1,128]{1,0:T(1,128)}, u32[]{:S(2)}) copy-start(f32[1,128]{1,0:T(1,128)} %get-tuple-element.5) | copy-start | bytes 1540

commit v4 on v3

--- a/solution.py
+++ b/solution.py
@@ -47,10 +47,14 @@
     source, lane = index_grids()
     tap = jnp.where(lane <= 10, lane + 10, lane - 118)
     used = (lane <= 10) | (lane >= 118)
+    rows[0] = jnp.zeros((128, 128), F32)
+    for k in range(taps.shape[0]):
+        rows[0, 2 * k : 2 * k + 2, :] = taps[k].astype(F32)
+    lines = rows[0].T.astype(BF16)
     for m in range(4):
-        wanted = (20 - tap if m % 2 else tap) + 21 * (m // 2)
+        wanted = 2 * (20 - tap if m % 2 else tap) + m // 2
         pick = jnp.where(used & (source == wanted), 1.0, 0.0).astype(BF16)
-        rows[m] = dot(taps[...], pick)
+        rows[m] = dot(lines, pick)
 
 
 def stamp_order(patch, band, gain, weight, ints, floats):
@@ -63,7 +67,7 @@
     def total(grid):
         return jnp.sum(grid, 0, keepdims=True)
 
-    where = across(patch[...])
+    where = across(patch[...]).T
     dz = lax.rem(where // 4 - z + 4, 4)
     dx = lax.rem(lax.rem(where, 4) - x + 4, 4)
     offset = dz * 4 + dx
@@ -180,12 +184,19 @@
                 (far, 1, three + 3),
                 (sides[1], diag_half, diag + 3),
                 (straight, late, two),
-                (link, early, one + early * 3),
-                (link, late, one + late * 3),
             ],
             1,
         ):
             row.append(send(k, tiles.at[span(offset, h)], got.at[dst : dst + 3], ssem.at[k, n], rsem.at[k, n]))
+        for n, (tile, dst, count) in enumerate(
+            [
+                (span(link, early).start, one + early * 3, 2),
+                (span(link, early).start + 2, one + early * 3 + 2, 1),
+                (span(link, late).start, one + late * 3, 3),
+            ],
+            6,
+        ):
+            row.append(send(k, tiles.at[tile : tile + count], got.at[dst : dst + count], ssem.at[k, n], rsem.at[k, n]))
         copies.append(row)
         info.append((far, straight, sides, diag_half, early, late, diag, three, two, one))
 
@@ -193,19 +204,19 @@
 
 
 def main_kernel(patch_of, band_of, gain_of, weight_of, taps, sky, pix, out, rms,
-                got, tiles, pixv, seg, carry, mats, blur, resi, back, skyb, rows, intv, floatv, ints, floats, held, held2,
+                got, tiles, pixv, seg, carry, mats, blur, resi, skyb, rows, intv, floatv, ints, floats, held, held2,
                 lsem, ssem, rsem, ssem2, rsem2, tsem, tsem2, tsem3, tsem4, early, free):
+    sky_load = pltpu.make_async_copy(sky, skyb, lsem.at[0])
+    sky_load.start()
     patch, exp = lax.axis_index("patch"), lax.axis_index("exp")
     peers = [{"patch": lax.rem(patch + k, 16)} for k in range(1, 16)]
     peers2 = [{"exp": lax.rem(exp + k, 8)} for k in range(1, 8)]
     barrier = pltpu.get_barrier_semaphore()
     for peer in peers + peers2:
         pl.semaphore_signal(barrier, inc=1, device_id=peer, device_id_type=MESH)
-    sky_load = pltpu.make_async_copy(sky, skyb, lsem.at[0])
-    sky_load.start()
     pix_load = pltpu.make_async_copy(pix, pixv, lsem.at[1])
+    sky_load.wait()
     pix_load.start()
-    sky_load.wait()
 
     @pl.loop(0, BANDS)
     def _(b):
@@ -250,9 +261,9 @@
             predicted = g[u] * dot(mats[u, 0], blur[u])
             resi[u] = (w[u] * (predicted - pixv[idx[u]].astype(F32))).astype(BF16)
         for u in range(PER):
-            back[u] = dot(mats[u, 1], resi[u]).astype(BF16)
+            blur[u] = dot(mats[u, 1], resi[u]).astype(BF16)
         for u in range(PER):
-            total = carry[...] * floats[0, at[u]] + g[u] * dot(back[u], mats[u, 2])
+            total = carry[...] * floats[0, at[u]] + g[u] * dot(blur[u], mats[u, 2])
             carry[...] = total
             seg[at[u]] = total.astype(BF16)
         return nothing
@@ -340,7 +351,10 @@
     pl.semaphore_wait(free, 4)
     for k in range(4):
         copies[k][0].start()
-    collect(9, 15)
+    collect(9, 11)
+    for k in range(4):
+        copies[k][4].start()
+    collect(11, 15)
     for k in range(4):
         copies[k][0].wait_recv()
         first = UNIT[info[k][0]] * BANDS
@@ -350,10 +364,19 @@
             r = slice(k * 64, k * 64 + 64)
             tiles[first + b, r] = (tiles[first + b, r].astype(F32) + got[b, r].astype(F32)).astype(BF16)
 
-        for n in (2, 3, 4):
+        for n in (2, 3):
             copies[k][n].start()
     collect(0, 5)
     collect(7, 9)
+    for n in (1, 4):
+        for k in range(4):
+            sides, diag_half = info[k][2:4]
+            copies[k][n].wait_recv()
+            dz, dx = sides[n // 4]
+            target = (dz, 0) if LINKS[k][0] == 0 else (0, dx)
+            add_into(span(target, diag_half), info[k][6] + n // 4 * HALF)
+    for k in range(4):
+        copies[k][6].start()
     for h in range(2):
         for k in range(4):
             copies[k][2 + h].wait_recv()
@@ -362,22 +385,14 @@
         for k in range(4):
             if info[k][5] == h:
                 copies[k][5].start()
-    for k in range(4):
-        sides, diag_half = info[k][2:4]
-        for s in range(2):
-            copies[k][1 if s == 0 else 4].wait_recv()
-            dz, dx = sides[s]
-            target = (dz, 0) if LINKS[k][0] == 0 else (0, dx)
-            add_into(span(target, diag_half), info[k][6] + s * HALF)
-    for k in range(4):
-        copies[k][6].start()
+                copies[k][7].start()
     for k in range(4):
         copies[k][5].wait_recv()
         add_into(span(LINKS[k], info[k][5]), info[k][8])
-        copies[k][7].start()
-    for k in range(4):
-        copies[k][6].wait_recv()
-        copies[k][7].wait_recv()
+        copies[k][8].start()
+    for k in range(4):
+        for n in (6, 7, 8):
+            copies[k][n].wait_recv()
 
     def finish(b, total):
         gradient = tiles[b].astype(F32)
@@ -441,7 +456,6 @@
             pltpu.VMEM((PER, 4, TS, TS), BF16),
             pltpu.VMEM((PER, TS, TS), BF16),
             pltpu.VMEM((PER, TS, TS), BF16),
-            pltpu.VMEM((PER, TS, TS), BF16),
             pltpu.VMEM((BANDS, TS, TS), F32),
             pltpu.VMEM((4, 128, 128), F32),
             pltpu.VMEM((8, 128), jnp.int32),
@@ -453,8 +467,8 @@
             pltpu.SemaphoreType.DMA((4,)),
             pltpu.SemaphoreType.DMA((4, 8)),
             pltpu.SemaphoreType.DMA((4, 8)),
-            pltpu.SemaphoreType.DMA((4, 8)),
-            pltpu.SemaphoreType.DMA((4, 8)),
+            pltpu.SemaphoreType.DMA((4, 9)),
+            pltpu.SemaphoreType.DMA((4, 9)),
             pltpu.SemaphoreType.DMA((15,)),
             pltpu.SemaphoreType.DMA((15,)),
             pltpu.SemaphoreType.DMA((7,)),
@@ -473,9 +487,11 @@
     sky_model, stamp_pixels, stamp_patch, stamp_band, psf_taps, stamp_gain, stamp_weight
 ):
     sky = sky_model.reshape(BANDS, TS, TS)
-    taps = jnp.pad(psf_taps.reshape(STAMPS, -1), ((0, 0), (0, 128 - 2 * psf_taps.shape[-1])))
-    band, gain, weight = (v.reshape(1, STAMPS) for v in (stamp_band, stamp_gain, stamp_weight))
-    new_model, rms = step(stamp_patch, band, gain, weight, taps, sky, stamp_pixels)
+    taps = psf_taps.transpose(2, 1, 0)
+    patch, band, gain, weight = (
+        v.reshape(1, STAMPS) for v in (stamp_patch, stamp_band, stamp_gain, stamp_weight)
+    )
+    new_model, rms = step(patch, band, gain, weight, taps, sky, stamp_pixels)
     return (new_model.reshape(sky_model.shape), rms[0, 0])
 
 

time: 158 us -> 155 us (0.981)
  local copies, waits for them, and re-layouts: 5.59 us -> 2.74 us
    unnamed x5 -> x3, local copies, waits for them, and re-layouts: 4.84 us -> 2.74 us
where the time goes in v4:
time: 155 us
  Pallas kernels  150 us (97%)
  local copies, waits for them, and re-layouts  2.74 us (2%)
  between operations  1.81 us (1%)
    pallas_call x1, Pallas kernels, step(): pl.pallas_call(main_kernel, out_shape=(jax.ShapeDtypeStruct((BANDS, TS, T...  150 us

profile of v4, /device:TPU:1, one launch (start us, length us, event | category | flops | bytes accessed | tf_op | source)
XLA Modules:
  0.0 154.8 jit_solution(16861506390470130386)
XLA Ops:
  0.6 150.3 %step.1 = (f32[6,256,256]{2,1,0:T(8,128)}, f32[1,128]{1,0:T(1,128)}) custom-call(s32[1,128]{1,0:T(1,128)} %bitcast.12, s32[1,128]{1,0:T(1,128)} %bitcast.13, bf16[1,128]{1,0:T(2,128)(2,1)} %bitcast.14, bf16[1,128]{1,0:T(2,128)(2,1)} %bitcast.15, bf16[21,2,128]{2,1,0:T(2,128)(2,1)} %bitcast.11, f32[6,256,256]{2,1,0:T(8,128)} %bitcast.10, ...), custom_call_target="tpu_custom_call" | custom-call | tf_op jit(solution)/shard_map/step/pallas_call | solution.py:442
  150.9 0.0 copy-start
  150.9 2.7 %copy.11 = f32[1,1,6,256,256]{4,3,2,1,0:T(8,128)} copy(f32[1,1,6,256,256]{4,3,2,1,0:T(8,128)} %bitcast.9) | data formatting | bytes 3145728
  153.6 0.0 copy-done
Async XLA Ops:
  150.9 2.7 %copy-start = (f32[1,128]{1,0:T(1,128)S(1)}, f32[1,128]{1,0:T(1,128)}, u32[]{:S(2)}) copy-start(f32[1,128]{1,0:T(1,128)} %get-tuple-element.5) | copy-start | bytes 1540

commit v5 on v4

--- a/solution.py
+++ b/solution.py
@@ -212,11 +212,11 @@
     peers = [{"patch": lax.rem(patch + k, 16)} for k in range(1, 16)]
     peers2 = [{"exp": lax.rem(exp + k, 8)} for k in range(1, 8)]
     barrier = pltpu.get_barrier_semaphore()
-    for peer in peers + peers2:
+    greeted = [{"patch": neighbour(link)} for link in LINKS] + peers2
+    for peer in greeted:
         pl.semaphore_signal(barrier, inc=1, device_id=peer, device_id_type=MESH)
     pix_load = pltpu.make_async_copy(pix, pixv, lsem.at[1])
     sky_load.wait()
-    pix_load.start()
 
     @pl.loop(0, BANDS)
     def _(b):
@@ -224,7 +224,7 @@
         got[b] = half
         tiles[b] = half
 
-    pl.semaphore_wait(barrier, len(peers) + len(peers2))
+    pl.semaphore_wait(barrier, len(greeted))
     moves = gather_copies(got, ssem, rsem)
     for k, link in enumerate(LINKS):
         for n in (0, 1) if link[0] == 0 else (1, 0):
@@ -237,6 +237,7 @@
     for c in tables:
         c.start()
     tap_rows(taps, rows)
+    pix_load.start()
     carry[...] = jnp.zeros_like(carry)
     mats[...] = jnp.zeros_like(mats)
 

time: 155 us -> 154 us (level)
  no operation moved by 1% of the time
where the time goes in v5:
time: 154 us
  Pallas kernels  149 us (97%)
  local copies, waits for them, and re-layouts  2.74 us (2%)
  between operations  1.81 us (1%)
    pallas_call x1, Pallas kernels, step(): pl.pallas_call(main_kernel, out_shape=(jax.ShapeDtypeStruct((BANDS, TS, T...  149 us

profile of v5, /device:TPU:1, one launch (start us, length us, event | category | flops | bytes accessed | tf_op | source)
XLA Modules:
  0.0 153.8 jit_solution(7910712559422749209)
XLA Ops:
  0.6 149.3 %step.1 = (f32[6,256,256]{2,1,0:T(8,128)}, f32[1,128]{1,0:T(1,128)}) custom-call(s32[1,128]{1,0:T(1,128)} %bitcast.12, s32[1,128]{1,0:T(1,128)} %bitcast.13, bf16[1,128]{1,0:T(2,128)(2,1)} %bitcast.14, bf16[1,128]{1,0:T(2,128)(2,1)} %bitcast.15, bf16[21,2,128]{2,1,0:T(2,128)(2,1)} %bitcast.11, f32[6,256,256]{2,1,0:T(8,128)} %bitcast.10, ...), custom_call_target="tpu_custom_call" | custom-call | tf_op jit(solution)/shard_map/step/pallas_call | solution.py:443
  149.9 0.0 copy-start
  149.9 2.7 %copy.11 = f32[1,1,6,256,256]{4,3,2,1,0:T(8,128)} copy(f32[1,1,6,256,256]{4,3,2,1,0:T(8,128)} %bitcast.9) | data formatting | bytes 3145728
  152.7 0.0 copy-done
Async XLA Ops:
  149.9 2.7 %copy-start = (f32[1,128]{1,0:T(1,128)S(1)}, f32[1,128]{1,0:T(1,128)}, u32[]{:S(2)}) copy-start(f32[1,128]{1,0:T(1,128)} %get-tuple-element.5) | copy-start | bytes 1540

commit v6 on v5

--- a/solution.py
+++ b/solution.py
@@ -395,18 +395,16 @@
         for n in (6, 7, 8):
             copies[k][n].wait_recv()
 
-    def finish(b, total):
+    def step_of(b):
         gradient = tiles[b].astype(F32)
         for k in range(4):
             gradient = gradient + got[info[k][9] + b].astype(F32)
-        step_field = STEP_RATE * gradient
-        skyb[b] = skyb[b] - step_field
+        return STEP_RATE * gradient
+
+    def square(b, total):
+        step_field = step_of(b)
         squares = (step_field * step_field).reshape(TS // 8, 8, TS).sum(0)
         return total + squares[:, :128] + squares[:, 128:]
-
-    squares = lax.fori_loop(0, BANDS, finish, jnp.zeros((8, 128), F32))
-    c = pltpu.make_async_copy(skyb, out, lsem.at[0])
-    c.start()
 
     def exchange(slots, place, value, devices, send_sems, recv_sems):
         slots[place] = value
@@ -423,17 +421,32 @@
         ]
         for share in shares:
             share.start()
-        for share in shares:
-            share.wait()
-        return jnp.sum(slots[...], 0)
-
-    squares = exchange(held, patch, squares, peers, tsem, tsem2)
-    squares = exchange(held2, exp, squares, peers2, tsem3, tsem4)
+        return shares
+
+    squares = lax.fori_loop(0, BANDS, square, jnp.zeros((8, 128), F32))
+    shares = exchange(held, patch, squares, peers, tsem, tsem2)
+
+    @pl.loop(0, BANDS)
+    def _(b):
+        skyb[b] = skyb[b] - step_of(b)
+
+    c = pltpu.make_async_copy(skyb, out, lsem.at[0])
+    c.start()
+    for share in shares:
+        share.wait_recv()
+    shares2 = exchange(held2, exp, jnp.sum(held[...], 0), peers2, tsem3, tsem4)
+    for share in shares:
+        share.wait_send()
+    for k in range(4):
+        for c2 in copies[k]:
+            c2.wait_send()
+    for share in shares2:
+        share.wait_recv()
+    squares = jnp.sum(held2[...], 0)
     mean = jnp.sum(jnp.sum(squares, 0, keepdims=True), 1, keepdims=True) / (128 * BANDS * TS * TS)
     rms[...] = jnp.broadcast_to(jnp.sqrt(mean + 1e-06), rms.shape)
-    for k in range(4):
-        for c2 in copies[k]:
-            c2.wait_send()
+    for share in shares2:
+        share.wait_send()
     c.wait()
 
 

time: 154 us -> 154 us (level)
  no operation moved by 1% of the time
where the time goes in v6:
time: 154 us
  Pallas kernels  149 us (97%)
  local copies, waits for them, and re-layouts  2.74 us (2%)
  between operations  1.81 us (1%)
    pallas_call x1, Pallas kernels, step(): pl.pallas_call(main_kernel, out_shape=(jax.ShapeDtypeStruct((BANDS, TS, T...  149 us

profile of v6, /device:TPU:1, one launch (start us, length us, event | category | flops | bytes accessed | tf_op | source)
XLA Modules:
  0.0 153.9 jit_solution(10437377596389659872)
XLA Ops:
  0.6 149.4 %step.1 = (f32[6,256,256]{2,1,0:T(8,128)}, f32[1,128]{1,0:T(1,128)}) custom-call(s32[1,128]{1,0:T(1,128)} %bitcast.12, s32[1,128]{1,0:T(1,128)} %bitcast.13, bf16[1,128]{1,0:T(2,128)(2,1)} %bitcast.14, bf16[1,128]{1,0:T(2,128)(2,1)} %bitcast.15, bf16[21,2,128]{2,1,0:T(2,128)(2,1)} %bitcast.11, f32[6,256,256]{2,1,0:T(8,128)} %bitcast.10, ...), custom_call_target="tpu_custom_call" | custom-call | tf_op jit(solution)/shard_map/step/pallas_call | solution.py:456
  150.0 0.0 copy-start
  150.0 2.7 %copy.11 = f32[1,1,6,256,256]{4,3,2,1,0:T(8,128)} copy(f32[1,1,6,256,256]{4,3,2,1,0:T(8,128)} %bitcast.9) | data formatting | bytes 3145728
  152.8 0.0 copy-done
Async XLA Ops:
  150.0 2.7 %copy-start = (f32[1,128]{1,0:T(1,128)S(1)}, f32[1,128]{1,0:T(1,128)}, u32[]{:S(2)}) copy-start(f32[1,128]{1,0:T(1,128)} %get-tuple-element.5) | copy-start | bytes 1540
